TPU v7x, 32 devices: a whole 2x2x4 slice. The times are simulated.
32 devices in a mesh: dp: 4 (over y, x), row: 2 (over core), col: 4 (over z).
Axes of the slice: x: 2, y: 2, z: 4, core: 2. Of those that a mesh axis runs over, the one named last changes fastest.
Arguments:
- inputs: bfloat16 [16384, 2048], P(('dp', 'col'), 'row'), may hold values from -6 to 6
- cotangent: bfloat16 [16384, 2048], P(('dp', 'col'), 'row'), may hold values from -6 to 6
- w_qkv: float32 [16, 128, 3, 16, 128], P('row', 'dp', None, 'col'), may hold values from -0.125 to 0.125
- w_out: float32 [16, 128, 2048], P('col', 'dp', 'row'), may hold values from -0.125 to 0.125
- w_gate_up: float32 [16, 128, 2, 8192], P('row', 'dp', None, 'col'), may hold values from -0.125 to 0.125
- w_down: float32 [64, 128, 2048], P('col', 'dp', 'row'), may hold values from -0.0625 to 0.0625
- gains: float32 [4, 2048], replicated, may hold values from 0.3 to 2.4, as said below
- gain_state: float32 [4, 2048], replicated, may hold values from 16384 to 98304, as said below
- row_state: float32 [14336], replicated, may hold values from 4915.2 to 98304, as said below
- col_state: float32 [26624], replicated, may hold values from 4915.2 to 98304, as said below
- positions: int32 [16, 1024], P(('dp', 'row')), may hold values from 0 to 1023, as said below
- block_map: int32 [16, 4], P(('dp', 'row')), may hold values from 0 to 3, as said below
Outputs:
- output: float32 [16384, 2048], P(('dp', 'col'), 'row')
- grad_inputs: float32 [16384, 2048], P(('dp', 'col'), 'row')
- grad_qkv: float32 [16, 128, 3, 16, 128], P('row', 'dp', None, 'col')
- grad_out: float32 [16, 128, 2048], P('col', 'dp', 'row')
- grad_gate_up: float32 [16, 128, 2, 8192], P('row', 'dp', None, 'col')
- grad_down: float32 [64, 128, 2048], P('col', 'dp', 'row')
- new_qkv: float32 [16, 128, 3, 16, 128], P('row', 'dp', None, 'col')
- new_out: float32 [16, 128, 2048], P('col', 'dp', 'row')
- new_gate_up: float32 [16, 128, 2, 8192], P('row', 'dp', None, 'col')
- new_down: float32 [64, 128, 2048], P('col', 'dp', 'row')
- copy_qkv: bfloat16 [16, 128, 3, 16, 128], P('row', 'dp', None, 'col')
- copy_out: bfloat16 [16, 128, 2048], P('col', 'dp', 'row')
- copy_gate_up: bfloat16 [16, 128, 2, 8192], P('row', 'dp', None, 'col')
- copy_down: bfloat16 [64, 128, 2048], P('col', 'dp', 'row')
- new_row_state: float32 [14336], replicated
- new_col_state: float32 [26624], replicated
- gain_grad: float32 [4, 2048], replicated
- new_gain_state: float32 [4, 2048], replicated
- new_gains: float32 [4, 2048], replicated
Inputs may be any that keep to these rules, and one draw needn't show every extreme that they name: Within a sequence positions count up by one from 0 and restart at 0 where a new document begins; every sequence begins with 0. `block_map`: entry b of a sequence's row is at most b. `gains`: Positive. `gain_state`: Positive. `row_state`: Positive. `col_state`: Positive.
All inputs are finite; a program needn't handle non-finite values.
Results may differ from a plain program's by a relative error of at most 0.019.
The roundings to bfloat16 on the way count: a program that leaves them out, or rounds other values in their place, can miss the bound.
Values may be sent and summed in bfloat16 or wider, within the bound.
No kernel may reach another device: no remote copies, remote signals or barrier semaphores. Data moves between devices by JAX's collectives and lax.ppermute only.
A program may use at most 384 MiB of HBM per device.

v0:
```python
import functools
import math

import jax
import jax.numpy as jnp
import numpy as np
from jax import lax
from jax.experimental import pallas as pl
from jax.experimental.pallas import tpu as pltpu
from jax.sharding import PartitionSpec as P

D = 2048
H = 16
HD = 128
FF = 8192
STEP = 3


EPSILON = 1e-06
TINY_SQUARE = 1e-30
ROPE_BASE = 500000.0
NEGATIVE = -1e30
CLIP_LEVEL = 0.5
GAIN_RATE = 0.3

LOW = jnp.bfloat16
FULL = jnp.float32


VMEM_LIMIT = 56 * 1024 * 1024


def dot(left, right):
    return jnp.dot(left, right, preferred_element_type=FULL)


def dot_back(left, right):
    return lax.dot_general(left, right, (((1,), (1,)), ((), ())), preferred_element_type=FULL)


def scaled_cost(flops, bytes_accessed, transcendentals, factor=2):
    return pl.CostEstimate(
        flops=factor * flops,
        bytes_accessed=factor * bytes_accessed,
        transcendentals=factor * transcendentals,
    )


def with_deps(kernel, count, deps):
    def body(*refs):
        return kernel(*refs[:count], *refs[count + len(deps) :])

    return body


def dep_specs(deps):
    return [pl.BlockSpec(memory_space=pl.ANY)] * len(deps)


def after(value, *others):
    if not others:
        return value

    def body(*refs):
        pass

    return pl.pallas_call(
        body,
        in_specs=dep_specs((value,) + others),
        out_specs=pl.BlockSpec(memory_space=pl.ANY),
        out_shape=jax.ShapeDtypeStruct(value.shape, value.dtype),
        input_output_aliases={0: 0},
        name="after",
    )(value, *others)


def kernel_params():
    return pltpu.CompilerParams(vmem_limit_bytes=VMEM_LIMIT)


def gate_kernel(h, gu_own, gu_other, hidden, by_gate, by_up):
    half = gu_own.shape[2]
    left = h[:, :half]
    right = h[:, half:]
    gate = dot(left, gu_own[0, 0]) + dot(right, gu_other[0, 0])
    up = dot(left, gu_own[0, 1]) + dot(right, gu_other[0, 1])
    sigmoid_gate = 1.0 / (1.0 + jnp.exp(-gate))
    silu = gate * sigmoid_gate
    hidden[...] = (silu * up).astype(LOW)
    by_gate[...] = (up * sigmoid_gate * (1.0 + gate * (1.0 - sigmoid_gate))).astype(LOW)
    by_up[...] = silu.astype(LOW)


def gate_forward(h, gu_own, gu_other, deps=()):
    tokens, width = h.shape
    n_col, _, half, mine = gu_own.shape
    weight = pl.BlockSpec((1, 2, half, mine), lambda j: (j, 0, 0, 0))
    piece = pl.BlockSpec((tokens, mine), lambda j: (0, j))
    shape = jax.ShapeDtypeStruct((tokens, n_col * mine), LOW)
    return pl.pallas_call(
        with_deps(gate_kernel, 3, deps),
        grid=(n_col,),
        in_specs=[pl.BlockSpec((tokens, width), lambda j: (0, 0)), weight, weight]
        + dep_specs(deps),
        out_specs=[piece, piece, piece],
        out_shape=[shape, shape, shape],
        cost_estimate=scaled_cost(
            flops=4 * tokens * width * n_col * mine,
            bytes_accessed=4 * gu_own.size + 2 * h.size + 6 * tokens * n_col * mine,
            transcendentals=tokens * n_col * mine,
        ),
        compiler_params=kernel_params(),
        name="gate_up",
    )(h, gu_own, gu_other, *deps)


def down_kernel(hidden, down_own, down_other, term):
    half = down_own.shape[1]
    term[:, :half] = dot(hidden[...], down_own[...]).astype(term.dtype)
    term[:, half:] = dot(hidden[...], down_other[...]).astype(term.dtype)


def down_forward(hidden, down_own, down_other, kind=LOW, deps=()):
    tokens, units = hidden.shape
    half = down_own.shape[1]
    rows = min(tokens, 256)
    weight = pl.BlockSpec((units, half), lambda i: (0, 0))
    return pl.pallas_call(
        with_deps(down_kernel, 3, deps),
        grid=(tokens // rows,),
        in_specs=[pl.BlockSpec((rows, units), lambda i: (i, 0)), weight, weight]
        + dep_specs(deps),
        out_specs=pl.BlockSpec((rows, 2 * half), lambda i: (i, 0)),
        out_shape=jax.ShapeDtypeStruct((tokens, 2 * half), kind),
        cost_estimate=scaled_cost(
            flops=4 * tokens * units * half,
            bytes_accessed=4 * down_own.size + 2 * hidden.size + 4 * tokens * half,
            transcendentals=0,
        ),
        compiler_params=kernel_params(),
        name="down",
    )(hidden, down_own, down_other, *deps)


def attended_back_kernel(grad, out_own, out_other, *results):
    half = out_own.shape[1]
    value = dot_back(grad[:, :half], out_own[...]) + dot_back(grad[:, half:], out_other[...])
    for k in range(len(results)):

        @pl.when(pl.program_id(0) == k)
        def _(k=k):
            results[k][0] = value.astype(LOW)


def attended_backward(grad, out_own, out_other, n_dp, deps):
    tokens, width = grad.shape
    rows, half = out_own.shape
    columns = rows // n_dp // 2
    weight = pl.BlockSpec((columns, half), lambda k, c: (2 * k + c, 0))

    def result_spec(i):
        return pl.BlockSpec(
            (1, tokens, columns), lambda k, c: (jnp.clip(2 * (k - i) + c, 0, 1), 0, 0)
        )

    return pl.pallas_call(
        with_deps(attended_back_kernel, 3, deps),
        grid=(n_dp, 2),
        in_specs=[pl.BlockSpec((tokens, width), lambda k, c: (0, 0)), weight, weight]
        + dep_specs(deps),
        out_specs=[result_spec(i) for i in range(n_dp)],
        out_shape=[jax.ShapeDtypeStruct((2, tokens, columns), LOW)] * n_dp,
        cost_estimate=scaled_cost(
            factor=3,
            flops=2 * grad.size * rows,
            bytes_accessed=4 * out_own.size + 2 * grad.size + 2 * tokens * rows,
            transcendentals=0,
        ),
        compiler_params=kernel_params(),
        name="attended_back",
    )(grad, out_own, out_other, *deps)


def mlp_back_kernel(
    m, by_gate, by_up, gu_own, gu_other, down_own, down_other, grad_gate, grad_up, term, total
):
    j = pl.program_id(0)
    half = gu_own.shape[2]
    grad_hidden = dot_back(m[:, :half], down_own[0]) + dot_back(m[:, half:], down_other[0])
    low_gate = (grad_hidden * by_gate[...].astype(FULL)).astype(LOW)
    low_up = (grad_hidden * by_up[...].astype(FULL)).astype(LOW)
    grad_gate[...] = low_gate
    grad_up[...] = low_up
    own = dot_back(low_gate, gu_own[0, 0]) + dot_back(low_up, gu_own[0, 1])
    other = dot_back(low_gate, gu_other[0, 0]) + dot_back(low_up, gu_other[0, 1])

    @pl.when(j == 0)
    def _():
        total[:, :half] = own
        total[:, half:] = other

    @pl.when(j > 0)
    def _():
        total[:, :half] += own
        total[:, half:] += other

    @pl.when(j == pl.num_programs(0) - 1)
    def _():
        term[...] = total[...].astype(LOW)


def mlp_backward(m, by_gate, by_up, gu_own, gu_other, down_own, down_other, deps=()):
    tokens, width = m.shape
    n_col, _, half, mine = gu_own.shape
    weight = pl.BlockSpec((1, 2, half, mine), lambda j: (j, 0, 0, 0))
    weight_down = pl.BlockSpec((1, mine, half), lambda j: (j, 0, 0))
    piece = pl.BlockSpec((tokens, mine), lambda j: (0, j))
    whole = pl.BlockSpec((tokens, width), lambda j: (0, 0))
    shape = jax.ShapeDtypeStruct((tokens, n_col * mine), LOW)
    return pl.pallas_call(
        with_deps(mlp_back_kernel, 7, deps),
        grid=(n_col,),
        in_specs=[whole, piece, piece, weight, weight, weight_down, weight_down]
        + dep_specs(deps),
        out_specs=[piece, piece, whole],
        out_shape=[shape, shape, jax.ShapeDtypeStruct((tokens, width), LOW)],
        scratch_shapes=[pltpu.VMEM((tokens, width), FULL)],
        cost_estimate=scaled_cost(
            flops=6 * tokens * width * n_col * mine,
            bytes_accessed=6 * gu_own.size + 4 * m.size + 8 * tokens * n_col * mine,
            transcendentals=0,
        ),
        compiler_params=kernel_params(),
        name="mlp_back",
    )(
        m,
        by_gate,
        by_up,
        gu_own,
        gu_other,
        down_own.reshape(n_col, mine, half),
        down_other.reshape(n_col, mine, half),
        *deps,
    )


def grad_kernel(count, groups, received, pieces, *refs):
    left = refs[:count]
    right = refs[count : count + count * groups]
    others = refs[count + count * groups : count + count * groups + received]
    results, turned = refs[-1 - pieces : -1], refs[-1]
    part = left[0].shape[0]
    step = pl.program_id(1)

    @pl.when(step == 0)
    def _():
        for k in range(count):
            turned[:, k * part : (k + 1) * part] = left[k][...].T

    for g in range(groups):
        total = None
        for k in range(count):
            term = dot(turned[:, k * part : (k + 1) * part], right[g * count + k][...])
            total = term if total is None else total + term
        if not received and pieces == 1:
            results[0][0, g] = total.astype(LOW)
        for n in range(max(received, pieces) if received or pieces > 1 else 0):

            @pl.when(step == n)
            def _(n=n):
                value = total + others[n][0, g].astype(FULL) if received else total
                results[n if pieces > 1 else 0][0, g] = value.astype(LOW)


def grad_block(
    left, left_at, rows, right, right_at, columns, steps, received, deps=(), factor=2, split=False
):
    count, groups = len(left), len(right)
    part = left[0].shape[0]
    tile = min(rows, 512)
    tiles = rows // tile
    left_spec = pl.BlockSpec((part, tile), lambda a, j: (0, left_at * tiles + a))
    right_spec = pl.BlockSpec((part, columns), lambda a, j: (0, right_at + j))
    share_spec = pl.BlockSpec((1, groups, tile, columns), lambda a, j: (0, 0, a, 0))
    result_spec = pl.BlockSpec((1, groups, tile, columns), lambda a, j: (j, 0, a, 0))
    operands = list(left) + [piece for group in right for piece in group] + list(received)
    specs = [left_spec] * count + [right_spec] * (count * groups) + [share_spec] * len(received)
    reads = len(operands)
    size = steps * groups * rows * columns
    pieces = steps if split else 1
    results = pl.pallas_call(
        with_deps(
            functools.partial(grad_kernel, count, groups, len(received), pieces), reads, deps
        ),
        grid=(tiles, steps),
        in_specs=specs + dep_specs(deps),
        out_specs=[share_spec if split else result_spec] * pieces,
        out_shape=[jax.ShapeDtypeStruct((steps // pieces, groups, rows, columns), LOW)] * pieces,
        scratch_shapes=[pltpu.VMEM((tile, count * part), LOW)],
        cost_estimate=scaled_cost(
            factor=factor,
            flops=2 * size * count * part,
            bytes_accessed=4 * size + 2 * count * part * (rows + steps * groups * columns * tiles),
            transcendentals=0,
        ),
        compiler_params=kernel_params(),
        name="weight_grad",
    )(*operands, *deps)
    return results if split else results[0]


def qkv_kernel(x, w_own, w_other, raw, squares, query_sum, key_sum):
    j = pl.program_id(1)
    half = w_own.shape[1]
    got = dot(x[0, :, :half], w_own[0]) + dot(x[0, :, half:], w_other[0])
    raw[0] = got
    query = got[:, :HD]
    key = got[:, HD : 2 * HD]

    @pl.when(j == 0)
    def _():
        query_sum[...] = query * query
        key_sum[...] = key * key

    @pl.when(j > 0)
    def _():
        query_sum[...] += query * query
        key_sum[...] += key * key

    @pl.when(j == pl.num_programs(1) - 1)
    def _():
        squares[0, 0:1] = jnp.sum(query_sum[...].T, axis=0, keepdims=True)
        squares[0, 1:2] = jnp.sum(key_sum[...].T, axis=0, keepdims=True)


def qkv_forward(x, w_own, w_other):
    shards_of, tokens, width = x.shape
    heads, half, columns = w_own.shape
    weight = pl.BlockSpec((1, half, columns), lambda k, j: (j, 0, 0))
    return pl.pallas_call(
        qkv_kernel,
        grid=(shards_of, heads),
        in_specs=[pl.BlockSpec((1, tokens, width), lambda k, j: (k, 0, 0)), weight, weight],
        out_specs=[
            pl.BlockSpec((1, tokens, columns), lambda k, j: (k, 0, j)),
            pl.BlockSpec((1, 2, tokens), lambda k, j: (k, 0, 0)),
        ],
        out_shape=[
            jax.ShapeDtypeStruct((shards_of, tokens, heads * columns), FULL),
            jax.ShapeDtypeStruct((shards_of, 2, tokens), FULL),
        ],
        scratch_shapes=[pltpu.VMEM((tokens, HD), FULL), pltpu.VMEM((tokens, HD), FULL)],
        cost_estimate=scaled_cost(
            flops=2 * x.size * heads * columns,
            bytes_accessed=2 * x.size + 4 * shards_of * w_own.size + 4 * shards_of * tokens * heads * columns,
            transcendentals=0,
        ),
        compiler_params=kernel_params(),
        name="qkv",
    )(x, w_own, w_other)


def token_scales(squares):
    return lax.rsqrt(squares[0] / D + EPSILON).T


def rope_kernel(raw, squares, cosine, sine_term, gain, packed):
    heads = gain.shape[1] // HD
    scales = token_scales(squares)
    for h in range(heads):
        core, at = h // (heads // 2), h % (heads // 2) * 3 * HD
        for n in range(2):
            value = raw[0, :, (3 * h + n) * HD : (3 * h + n + 1) * HD] * scales[:, n : n + 1]
            value = value * gain[n : n + 1, h * HD : (h + 1) * HD]
            turned = value * cosine[0] + pltpu.roll(value, HD // 2, 1) * sine_term[0]
            packed[core, 0, :, at + n * HD : at + (n + 1) * HD] = turned.astype(LOW)
        packed[core, 0, :, at + 2 * HD : at + 3 * HD] = raw[
            0, :, (3 * h + 2) * HD : (3 * h + 3) * HD
        ].astype(LOW)


def rope_specs(raw, gain):
    shards_of, tokens, columns = raw.shape
    return [
        pl.BlockSpec((1, tokens, columns), lambda k: (k, 0, 0)),
        pl.BlockSpec((1, 2, tokens), lambda k: (k, 0, 0)),
        pl.BlockSpec((1, tokens, HD), lambda k: (k, 0, 0)),
        pl.BlockSpec((1, tokens, HD), lambda k: (k, 0, 0)),
        pl.BlockSpec(gain.shape, lambda k: (0, 0)),
    ]


def rope_forward(raw, squares, cosine, sine_term, gain, deps=()):
    shards_of, tokens, columns = raw.shape
    return pl.pallas_call(
        with_deps(rope_kernel, 5, deps),
        grid=(shards_of,),
        in_specs=rope_specs(raw, gain) + dep_specs(deps),
        out_specs=pl.BlockSpec((2, 1, tokens, columns // 2), lambda k: (0, k, 0, 0)),
        out_shape=jax.ShapeDtypeStruct((2, shards_of, tokens, columns // 2), LOW),
        cost_estimate=scaled_cost(
            flops=8 * raw.size, bytes_accessed=6 * raw.size, transcendentals=0
        ),
        compiler_params=kernel_params(),
        name="rope",
    )(raw, squares, cosine, sine_term, gain, *deps)


def turned_back(grads, raw, cosine, sine_term, gain, scales, h, n):
    heads = gain.shape[1] // HD
    core, at = h // (heads // 2), (h % (heads // 2) * 3 + n) * HD
    value = grads[core, 0, :, at : at + HD].astype(FULL)
    value = value * cosine[0] - pltpu.roll(value, HD // 2, 1) * sine_term[0]
    normed = raw[0, :, (3 * h + n) * HD : (3 * h + n + 1) * HD] * scales[:, n : n + 1]
    return (value, normed, value * gain[n : n + 1, h * HD : (h + 1) * HD])


def rope_inner_kernel(raw, squares, cosine, sine_term, gain, grads, inner, gain_grad):
    heads = gain.shape[1] // HD
    scales = token_scales(squares)

    @pl.when(pl.program_id(0) == 0)
    def _():
        gain_grad[...] = jnp.zeros(gain_grad.shape, FULL)

    for n in range(2):
        total = None
        for h in range(heads):
            value, normed, scaled = turned_back(
                grads, raw, cosine, sine_term, gain, scales, h, n
            )
            term = normed * scaled
            total = term if total is None else total + term
            gain_grad[n : n + 1, h * HD : (h + 1) * HD] += jnp.sum(
                value * normed, axis=0, keepdims=True
            )
        inner[0, n : n + 1] = jnp.sum(total.T, axis=0, keepdims=True)


def rope_inner(raw, squares, cosine, sine_term, gain, grads, deps=()):
    shards_of, tokens, columns = raw.shape
    return pl.pallas_call(
        with_deps(rope_inner_kernel, 6, deps),
        grid=(shards_of,),
        in_specs=rope_specs(raw, gain)
        + [pl.BlockSpec((2, 1, tokens, columns // 2), lambda k: (0, k, 0, 0))]
        + dep_specs(deps),
        out_specs=[
            pl.BlockSpec((1, 2, tokens), lambda k: (k, 0, 0)),
            pl.BlockSpec(gain.shape, lambda k: (0, 0)),
        ],
        out_shape=[
            jax.ShapeDtypeStruct((shards_of, 2, tokens), FULL),
            jax.ShapeDtypeStruct(gain.shape, FULL),
        ],
        cost_estimate=scaled_cost(
            factor=4,
            flops=12 * raw.size, bytes_accessed=6 * raw.size, transcendentals=0
        ),
        compiler_params=kernel_params(),
        name="rope_inner",
    )(raw, squares, cosine, sine_term, gain, grads, *deps)


def rope_back_kernel(raw, squares, cosine, sine_term, gain, grads, inner, result):
    heads = gain.shape[1] // HD
    scales = token_scales(squares)
    means = (inner[0] / D).T
    for h in range(heads):
        for n in range(2):
            _, normed, scaled = turned_back(grads, raw, cosine, sine_term, gain, scales, h, n)
            value = scales[:, n : n + 1] * (scaled - normed * means[:, n : n + 1])
            result[0, :, (3 * h + n) * HD : (3 * h + n + 1) * HD] = value.astype(LOW)
        core, at = h // (heads // 2), (h % (heads // 2) * 3 + 2) * HD
        result[0, :, (3 * h + 2) * HD : (3 * h + 3) * HD] = grads[core, 0, :, at : at + HD]


def rope_backward(raw, squares, cosine, sine_term, gain, grads, inner, deps=()):
    shards_of, tokens, columns = raw.shape
    return pl.pallas_call(
        with_deps(rope_back_kernel, 7, deps),
        grid=(shards_of,),
        in_specs=rope_specs(raw, gain)
        + [
            pl.BlockSpec((2, 1, tokens, columns // 2), lambda k: (0, k, 0, 0)),
            pl.BlockSpec((1, 2, tokens), lambda k: (k, 0, 0)),
        ]
        + dep_specs(deps),
        out_specs=pl.BlockSpec((1, tokens, columns), lambda k: (k, 0, 0)),
        out_shape=jax.ShapeDtypeStruct((shards_of, tokens, columns), LOW),
        cost_estimate=scaled_cost(
            factor=4,
            flops=12 * raw.size, bytes_accessed=8 * raw.size, transcendentals=0
        ),
        compiler_params=kernel_params(),
        name="rope_back",
    )(raw, squares, cosine, sine_term, gain, grads, inner, *deps)


def qkv_back_kernel(grad, w_own, w_other, term):
    heads, half, columns = w_own.shape
    for part, weight in enumerate((w_own, w_other)):
        total = None
        for j in range(heads):
            value = dot_back(grad[:, j * columns : (j + 1) * columns], weight[j])
            total = value if total is None else total + value
        term[:, part * half : (part + 1) * half] = total.astype(LOW)


def qkv_backward(grad, w_own, w_other, deps=()):
    tokens, columns = grad.shape
    heads, half, _ = w_own.shape
    rows = min(tokens, 256)
    weight = pl.BlockSpec(w_own.shape, lambda i: (0, 0, 0))
    return pl.pallas_call(
        with_deps(qkv_back_kernel, 3, deps),
        grid=(tokens // rows,),
        in_specs=[pl.BlockSpec((rows, columns), lambda i: (i, 0)), weight, weight]
        + dep_specs(deps),
        out_specs=pl.BlockSpec((rows, 2 * half), lambda i: (i, 0)),
        out_shape=jax.ShapeDtypeStruct((tokens, 2 * half), LOW),
        cost_estimate=scaled_cost(
            factor=4,
            flops=4 * grad.size * half,
            bytes_accessed=4 * w_own.size + 2 * grad.size + 4 * tokens * half,
            transcendentals=0,
        ),
        compiler_params=kernel_params(),
        name="qkv_back",
    )(grad, w_own, w_other, *deps)


def swap(values, axis, step):
    count = lax.axis_size(axis)
    return lax.ppermute(values, axis, [(i, i ^ step) for i in range(count)])


def is_relative():
    return lax.axis_size("dp") == 4


def place_of(entry):
    if is_relative():
        return lax.axis_index("dp") ^ entry
    return entry


def gather_begin(values):
    if not is_relative():
        return ()
    return (swap(values, "dp", 1), swap(values, "dp", 2))


def gather_end(values, begun):
    if not is_relative():
        whole = lax.all_gather(values, "dp", axis=0)
        return [whole[k] for k in range(whole.shape[0])]
    first, second = begun
    half = first.shape[0] // 2
    third = jnp.concatenate([swap(second[:half], "dp", 1), swap(first[half:], "dp", 2)], axis=0)
    return [values, first, second, third]


def scatter_begin(parts):
    if not is_relative():
        return ()
    half = parts[0].shape[0] // 2
    _, first, second, third = parts
    return (
        swap(third[:half], "dp", 1),
        swap(third[half:], "dp", 2),
        swap(first[:half], "dp", 1),
        swap(second[half:], "dp", 2),
    )


def scatter_middle(parts, begun):
    if not is_relative():
        return ()
    half = parts[0].shape[0] // 2
    _, first, second, _ = parts
    low_third, high_third = begun[:2]
    return (
        swap((first[half:].astype(FULL) + high_third.astype(FULL)).astype(LOW), "dp", 1),
        swap((second[:half].astype(FULL) + low_third.astype(FULL)).astype(LOW), "dp", 2),
    )


def scatter_end(parts, begun, middle):
    if not is_relative():
        return lax.psum_scatter(jnp.stack(parts), "dp", scatter_dimension=0).astype(FULL)
    half = parts[0].shape[0] // 2
    own = parts[0].astype(FULL)
    first_low, second_high = begun[2:]
    first_high, second_low = middle
    return jnp.concatenate(
        [
            own[:half] + first_low.astype(FULL) + second_low.astype(FULL),
            own[half:] + first_high.astype(FULL) + second_high.astype(FULL),
        ],
        axis=0,
    )


def scatter_dp(parts):
    begun = scatter_begin(parts)
    return scatter_end(parts, begun, scatter_middle(parts, begun))


def trade_dp(parts):
    if not is_relative():
        traded = lax.all_to_all(jnp.stack(parts), "dp", 0, 0, tiled=True)
        return [traded[k] for k in range(traded.shape[0])]
    return [parts[0]] + [swap(parts[k], "dp", k) for k in range(1, 4)]


def exchange_dp(blocks):
    if not is_relative():
        return lax.all_to_all(blocks, "dp", 0, 0, tiled=True)
    me = lax.axis_index("dp")
    got = []
    for k in range(4):
        sent = lax.dynamic_index_in_dim(blocks, me ^ k, 0, keepdims=False)
        got.append(swap(sent, "dp", k) if k else sent)
    odd, far = me % 2 == 1, me >= 2
    first, second = jnp.where(odd, got[1], got[0]), jnp.where(odd, got[0], got[1])
    third, fourth = jnp.where(odd, got[3], got[2]), jnp.where(odd, got[2], got[3])
    return jnp.stack(
        [
            jnp.where(far, third, first),
            jnp.where(far, fourth, second),
            jnp.where(far, first, third),
            jnp.where(far, second, fourth),
        ]
    )


def exchange_row(blocks):
    other = 1 - lax.axis_index("row")
    sent = lax.dynamic_index_in_dim(blocks, other, 0, keepdims=True)
    return lax.dynamic_update_slice_in_dim(blocks, swap(sent, "row", 1), other, 0)


def sum_dp(values):
    if not is_relative():
        return lax.psum(values, "dp")
    one = swap(values, "dp", 1)
    values = values + jnp.stack([one[1], one[0], one[3], one[2]])
    two = swap(values, "dp", 2)
    return values + jnp.stack([two[2], two[3], two[0], two[1]])


def sum_all(values):
    for axis in ("row", "dp", "col"):
        step = 1
        while step < lax.axis_size(axis):
            values = values + swap(values, axis, step)
            step *= 2
    return values


def other_row(values):
    return swap(values, "row", 1)


def attend_kernel(starts, query, key, value, doc_key, doc_query, mixed, log_total):
    sequence = pl.program_id(0)
    parts, _, part, _ = query.shape
    length = parts * part
    nblock = starts.shape[1]
    block = length // nblock
    keys_in = key[...].reshape(length, HD)
    queries = query[...].reshape(length, HD)
    values_turned = value[...].reshape(length, HD).T
    scaling = HD ** (-0.5)
    for b in range(nblock):
        lo = b * block
        hi = lo + block
        scores = (
            lax.dot_general(
                keys_in[:hi],
                queries[lo:hi],
                (((1,), (1,)), ((), ())),
                preferred_element_type=FULL,
            )
            * scaling
        )
        place = lax.broadcasted_iota(jnp.int32, (hi, 1), 0)
        group = jnp.where(place >= starts[sequence, b] * block, doc_key[0, :hi, :], -1)
        scores = jnp.where(group == doc_query[0, :, lo:hi], scores, NEGATIVE)
        highest = jnp.max(scores, axis=0, keepdims=True)
        exponent = jnp.exp(scores - highest)
        total = jnp.sum(exponent, axis=0, keepdims=True)
        probability = (exponent * (1.0 / total)).astype(LOW)
        turned = jnp.dot(values_turned[:, :hi], probability, preferred_element_type=FULL)
        at = lo // part
        mixed[at, 0, lo - at * part : hi - at * part, :] = turned.T.astype(LOW)
        log_total[0, 0, :, lo:hi] = highest + jnp.log(total)


def attend_back_kernel(
    starts, query, key, value, grad_mixed, doc_key, doc_query, log_total, grads, grad_key, grad_value
):
    sequence = pl.program_id(0)
    head = pl.program_id(1)
    parts, _, part, _ = query.shape
    length = parts * part
    nblock = starts.shape[1]
    block = length // nblock
    keys_in = key[...].reshape(length, HD)
    queries = query[...].reshape(length, HD)
    values = value[...].reshape(length, HD)
    upstream = grad_mixed[...].reshape(length, HD)
    keys_turned = keys_in.T
    scaling = HD ** (-0.5)
    query_at = pl.ds(pl.multiple_of(3 * head * HD, HD), HD)
    for b in range(nblock - 1, -1, -1):
        lo = b * block
        hi = lo + block
        scores = (
            lax.dot_general(
                keys_in[:hi],
                queries[lo:hi],
                (((1,), (1,)), ((), ())),
                preferred_element_type=FULL,
            )
            * scaling
        )
        place = lax.broadcasted_iota(jnp.int32, (hi, 1), 0)
        group = jnp.where(place >= starts[sequence, b] * block, doc_key[0, :hi, :], -1)
        scores = jnp.where(group == doc_query[0, :, lo:hi], scores, NEGATIVE)
        probability = jnp.exp(scores - log_total[0, 0, :, lo:hi])
        term_value = jnp.dot(
            probability.astype(LOW), upstream[lo:hi], preferred_element_type=FULL
        )
        grad_prob = lax.dot_general(
            values[:hi], upstream[lo:hi], (((1,), (1,)), ((), ())), preferred_element_type=FULL
        )
        weighted = probability * grad_prob
        center = jnp.sum(weighted, axis=0, keepdims=True)
        grad_scores = (weighted - probability * center).astype(LOW)
        term_key = jnp.dot(grad_scores, queries[lo:hi], preferred_element_type=FULL)
        if b == nblock - 1:
            grad_value[...] = term_value
            grad_key[...] = term_key
        else:
            grad_value[:hi] += term_value
            grad_key[:hi] += term_key
        turned = jnp.dot(keys_turned[:, :hi], grad_scores, preferred_element_type=FULL) * scaling
        at = lo // part
        grads[at, 0, lo - at * part : hi - at * part, query_at] = turned.T.astype(LOW)
    key_at = pl.ds(pl.multiple_of((3 * head + 1) * HD, HD), HD)
    value_at = pl.ds(pl.multiple_of((3 * head + 2) * HD, HD), HD)
    grads[:, 0, :, key_at] = (grad_key[...] * scaling).astype(LOW).reshape(parts, part, HD)
    grads[:, 0, :, value_at] = grad_value[...].astype(LOW).reshape(parts, part, HD)


def attention_cost(packed, heads, products, factor):
    parts, nseq, part, _ = packed.shape
    pairs = nseq * heads * (parts * part) ** 2 * 5 // 8
    return scaled_cost(
        factor=factor, flops=2 * pairs * HD * products, bytes_accessed=2 * packed.size * 2, transcendentals=pairs
    )


def piece_spec(packed, stride, offset):
    parts, _, part, _ = packed.shape
    return pl.BlockSpec((parts, 1, part, HD), lambda s, h, *_: (0, s, 0, stride * h + offset))


def attend_forward(packed, starts, documents):
    parts, nseq, part, width = packed.shape
    heads = width // (3 * HD)
    length = parts * part
    return pl.pallas_call(
        attend_kernel,
        grid_spec=pltpu.PrefetchScalarGridSpec(
            num_scalar_prefetch=1,
            grid=(nseq, heads),
            in_specs=[
                piece_spec(packed, 3, 0),
                piece_spec(packed, 3, 1),
                piece_spec(packed, 3, 2),
                pl.BlockSpec((1, length, 1), lambda s, h, *_: (s, 0, 0)),
                pl.BlockSpec((1, 1, length), lambda s, h, *_: (s, 0, 0)),
            ],
            out_specs=[
                piece_spec(packed, 1, 0),
                pl.BlockSpec((1, 1, 1, length), lambda s, h, *_: (s, h, 0, 0)),
            ],
        ),
        out_shape=[
            jax.ShapeDtypeStruct((parts, nseq, part, heads * HD), LOW),
            jax.ShapeDtypeStruct((nseq, heads, 1, length), FULL),
        ],
        cost_estimate=attention_cost(packed, heads, 2, 2),
        compiler_params=pltpu.CompilerParams(vmem_limit_bytes=48 * 1024 * 1024),
        name="attend",
    )(starts, packed, packed, packed, documents[:, :, None], documents[:, None, :])


def attend_backward(packed, starts, documents, log_total, grad_mixed, deps=()):
    parts, nseq, part, width = packed.shape
    heads = width // (3 * HD)
    length = parts * part
    return pl.pallas_call(
        with_deps(attend_back_kernel, 8, deps),
        grid_spec=pltpu.PrefetchScalarGridSpec(
            num_scalar_prefetch=1,
            grid=(nseq, heads),
            in_specs=[
                piece_spec(packed, 3, 0),
                piece_spec(packed, 3, 1),
                piece_spec(packed, 3, 2),
                piece_spec(packed, 1, 0),
                pl.BlockSpec((1, length, 1), lambda s, h, *_: (s, 0, 0)),
                pl.BlockSpec((1, 1, length), lambda s, h, *_: (s, 0, 0)),
                pl.BlockSpec((1, 1, 1, length), lambda s, h, *_: (s, h, 0, 0)),
            ]
            + dep_specs(deps),
            out_specs=pl.BlockSpec((parts, 1, part, width), lambda s, h, *_: (0, s, 0, 0)),
            scratch_shapes=[pltpu.VMEM((length, HD), FULL), pltpu.VMEM((length, HD), FULL)],
        ),
        out_shape=jax.ShapeDtypeStruct(packed.shape, LOW),
        cost_estimate=attention_cost(packed, heads, 5, 5),
        compiler_params=pltpu.CompilerParams(vmem_limit_bytes=48 * 1024 * 1024),
        name="attend_back",
    )(
        starts,
        packed,
        packed,
        packed,
        grad_mixed,
        documents[:, :, None],
        documents[:, None, :],
        log_total,
        *deps,
    )


def angles(places):
    halfway = HD // 2
    frequency = ROPE_BASE ** (-jnp.arange(halfway, dtype=FULL) / halfway)
    turned = places.astype(FULL)[..., None] * jnp.concatenate([frequency, frequency])
    sign = jnp.where(jnp.arange(HD) < halfway, -1.0, 1.0)
    return (jnp.cos(turned), jnp.sin(turned) * sign)


def norm_back(upstream, normed, scaling, gain):
    scaled = upstream * gain
    inner = jnp.mean(normed * scaled, axis=1, keepdims=True)
    return (scaling * (scaled - normed * inner), jnp.sum(upstream * normed, axis=0))


def placed(shape, piece, starts):
    return lax.dynamic_update_slice(jnp.zeros(shape, FULL), piece, starts).reshape(-1)


def sequence_span(length, tokens):
    return max(1, length // tokens)


def regroup(values, span):
    if span == 1:
        return values
    n_dp, n_col = lax.axis_size("dp"), lax.axis_size("col")
    moves = []
    for i in range(n_dp):
        for j in range(n_col):
            to_i = i - i % span + j % span
            to_j = j - j % span + i % span
            moves.append((i * n_col + j, to_i * n_col + to_j))
    return lax.ppermute(values, ("dp", "col"), moves)


def heads_line_up():
    return H // lax.axis_size("col") == lax.axis_size("dp")


def fetch_qkv(low, deps):
    nb, inner, three, heads, _ = low.shape
    n_dp = lax.axis_size("dp")
    if not heads_line_up():
        whole = lax.all_gather(low, "dp", axis=1, tiled=True)
        whole = lax.all_gather(whole, "col", axis=3, tiled=True)
        mine = H // n_dp
        whole = lax.dynamic_slice_in_dim(whole, lax.axis_index("dp") * mine, mine, 3)
        return whole.transpose(3, 0, 1, 2, 4).reshape(mine, nb * HD, three * HD)
    sent = low.transpose(3, 0, 1, 2, 4).reshape(heads, nb * inner, three * HD)
    got = exchange_dp(after(sent, *deps)).reshape(n_dp, nb, inner, three * HD).transpose(1, 0, 2, 3)
    got = got.reshape(nb * HD, three * HD)
    return lax.all_gather(got, "col", axis=0)


def fetch_out(low):
    heads, inner, cols = low.shape
    if not heads_line_up():
        whole = lax.all_gather(low, "dp", axis=1, tiled=True)
        return lax.all_gather(whole, "col", axis=0, tiled=True).reshape(D, cols)
    got = exchange_dp(low).reshape(HD, cols)
    return lax.all_gather(got, "col", axis=0).reshape(heads * HD, cols)


def send_gate_up(weight):
    nb, inner, two, cols = weight.shape
    n_dp = lax.axis_size("dp")
    mine = cols // n_dp
    sent = weight.astype(LOW).reshape(nb, inner, two, n_dp, mine).transpose(3, 2, 0, 1, 4)
    return sent.reshape(n_dp, two * nb * inner, mine)


def fetch_gate_up(sent, shape):
    nb, inner, two, cols = shape
    n_dp = lax.axis_size("dp")
    mine = cols // n_dp
    got = exchange_dp(sent)
    got = got.reshape(n_dp, two, nb, inner, mine).transpose(1, 2, 0, 3, 4)
    got = got.reshape(two, nb * HD, mine)
    return (lax.all_gather(got, "col", axis=0), got)


def send_down(weight):
    blocks, inner, cols = weight.shape
    n_dp = lax.axis_size("dp")
    return weight.astype(LOW).reshape(n_dp, blocks // n_dp * inner, cols)


def fetch_down(sent, shape):
    blocks, inner, cols = shape
    n_dp, n_col = lax.axis_size("dp"), lax.axis_size("col")
    mine = blocks // n_dp
    got = exchange_dp(sent)
    got = got.reshape(n_dp, mine, inner, cols).transpose(1, 0, 2, 3).reshape(mine * HD, cols)
    return (lax.all_gather(got, "col", axis=0).reshape(n_col * mine * HD, cols), got)


def reduce_col(values):
    return lax.psum_scatter(values, "col", scatter_dimension=0)


def grad_for_other(left, rows, right, columns, steps, by_rows, deps=(), factor=2):
    places = (1, 0) if by_rows else (0, 1)
    return grad_block(left, places[0], rows, right, places[1], columns, steps, (), deps, factor, True)


def grad_for_own(left, rows, right, columns, steps, received, deps=(), factor=2):
    received = [other_row(piece) for piece in received]
    return grad_block(left, 0, rows, right, 0, columns, steps, received, deps, factor)


def in_turn(order, call, results, deps=()):
    for k in order:
        results[k] = call(k, deps)
        last = results[k]
        deps = (last[0] if isinstance(last, (list, tuple)) else last,)
    return deps


def settle_qkv(half, shape):
    nb, inner, three, heads, _ = shape
    n_dp = lax.axis_size("dp")
    mine = H // n_dp
    if not heads_line_up():
        half = half.reshape(mine, nb, HD, three, HD).transpose(1, 2, 3, 0, 4)
        whole = lax.dynamic_update_slice_in_dim(
            jnp.zeros((nb, HD, three, H, HD), LOW), half, lax.axis_index("dp") * mine, 3
        )
        whole = lax.psum_scatter(whole, "dp", scatter_dimension=1, tiled=True)
        return lax.psum_scatter(whole, "col", scatter_dimension=3, tiled=True).astype(FULL)
    summed = half
    sent = summed.reshape(nb, n_dp, inner, three * HD).transpose(1, 0, 2, 3)
    got = exchange_dp(sent.reshape(n_dp, nb * inner, three * HD))
    return got.reshape(n_dp, nb, inner, three, HD).transpose(1, 2, 3, 0, 4).astype(FULL)


def settle_out(half, shape):
    heads, inner, cols = shape
    if not heads_line_up():
        whole = half.reshape(H, HD, cols)
        whole = lax.psum_scatter(whole, "dp", scatter_dimension=1, tiled=True)
        return lax.psum_scatter(whole, "col", scatter_dimension=0, tiled=True).astype(FULL)
    return exchange_dp(half.reshape(lax.axis_size("dp"), inner, cols)).astype(FULL)


def send_gate_up_grad(summed, shape):
    nb, inner, two, cols = shape
    n_dp = lax.axis_size("dp")
    mine = cols // n_dp
    sent = summed.reshape(two, nb, n_dp, inner, mine).transpose(2, 0, 1, 3, 4)
    return sent.reshape(n_dp, two * nb * inner, mine)


def gate_up_grad(got, shape):
    nb, inner, two, cols = shape
    n_dp = lax.axis_size("dp")
    got = got.reshape(n_dp, two, nb, inner, cols // n_dp).transpose(2, 3, 1, 0, 4)
    return got.reshape(shape).astype(FULL)


def send_down_grad(summed, shape):
    blocks, inner, cols = shape
    n_dp = lax.axis_size("dp")
    mine = blocks // n_dp
    sent = summed.reshape(mine, n_dp, inner, cols).transpose(1, 0, 2, 3)
    return sent.reshape(n_dp, mine * inner, cols)


DECAY = 1.0 - STEP ** (-0.8)


def square_sums(matrices):
    rows, cols = [], []
    for grad, _, row_shape, col_shape, row_at, col_at, _ in matrices:
        squares = grad * grad
        rows.append(placed(row_shape, jnp.sum(squares, axis=tuple(range(2, grad.ndim))), row_at))
        cols.append(placed(col_shape, jnp.sum(squares, axis=(0, 1)), col_at))
    return (jnp.concatenate(rows), jnp.concatenate(cols))


def spans(shapes):
    at, result = 0, []
    for shape in shapes:
        result.append((at, at + math.prod(shape)))
        at = result[-1][1]
    return result


def new_states(matrices, row_sums, col_sums, old_row, old_col):
    row_spans = spans([matrix[2] for matrix in matrices])
    col_spans = spans([matrix[3] for matrix in matrices])
    row_parts = np.concatenate(
        [np.full(b - a, 1.0 / (d - c), np.float32) for (a, b), (c, d) in zip(row_spans, col_spans)]
    )
    col_parts = np.concatenate(
        [np.full(d - c, 1.0 / (b - a), np.float32) for (a, b), (c, d) in zip(row_spans, col_spans)]
    )
    new_row = DECAY * old_row + (1.0 - DECAY) * (row_sums * row_parts + TINY_SQUARE)
    new_col = DECAY * old_col + (1.0 - DECAY) * (col_sums * col_parts + TINY_SQUARE)
    return (new_row, new_col)


def scaled_updates(matrices, new_row, new_col):
    row_spans = spans([matrix[2] for matrix in matrices])
    col_spans = spans([matrix[3] for matrix in matrices])
    updates, sizes = [], []
    for n, (grad, _, row_shape, col_shape, row_at, col_at, _) in enumerate(matrices):
        row_all = new_row[slice(*row_spans[n])]
        col_all = new_col[slice(*col_spans[n])]
        row_here = lax.dynamic_slice(row_all.reshape(row_shape), row_at, grad.shape[:2])
        col_here = lax.dynamic_slice(col_all.reshape(col_shape), col_at, grad.shape[2:])
        row_here = row_here.reshape(grad.shape[:2] + (1,) * (grad.ndim - 2))
        update = grad * lax.rsqrt(row_here * col_here[None, None] / jnp.mean(row_all))
        updates.append(update)
        sizes.append(jnp.sum(update * update))
    lane = lax.broadcasted_iota(jnp.int32, (8, 128), 1)
    packed = jnp.zeros((8, 128), FULL)
    for n, size in enumerate(sizes):
        packed = jnp.where(lane == n, size, packed)
    return (updates, packed)


def renew(matrices, updates, sizes):
    renewed = []
    for n, matrix in enumerate(matrices):
        count = math.prod(matrix[2]) * math.prod(matrix[3])
        clip = jnp.maximum(1.0, jnp.sqrt(sizes[0, n] / count) / CLIP_LEVEL)
        renewed.append(matrix[1] - matrix[-1] * updates[n] / clip)
    return renewed


def shards(
    inputs,
    cotangent,
    w_qkv,
    w_out,
    w_gate_up,
    w_down,
    gains,
    gain_state,
    row_state,
    col_state,
    positions,
    block_map,
):
    row_pos = lax.axis_index("row")
    col_pos = lax.axis_index("col")
    data_pos = lax.axis_index("dp")
    n_dp, n_col = lax.axis_size("dp"), lax.axis_size("col")
    length = positions.shape[1]
    chip_tokens = inputs.shape[0]
    tokens = chip_tokens // 2
    width = inputs.shape[1]
    span = sequence_span(length, chip_tokens)
    heads_here = H // n_dp
    local = heads_here * HD

    def enter(values):
        values = regroup(values, span)
        kept = lax.dynamic_slice_in_dim(values, row_pos * tokens, tokens, 0)
        sent = lax.dynamic_slice_in_dim(values, (1 - row_pos) * tokens, tokens, 0)
        return jnp.concatenate([kept, swap(sent, "row", 1)], axis=1)

    def leave(values):
        got = swap(values[:, width:], "row", 1)
        result = jnp.zeros((chip_tokens, width), values.dtype)
        result = lax.dynamic_update_slice_in_dim(result, values[:, :width], row_pos * tokens, 0)
        result = lax.dynamic_update_slice_in_dim(result, got, (1 - row_pos) * tokens, 0)
        return regroup(result, span)

    def own_first(vector):
        parts = vector.reshape(2, width)
        return jnp.concatenate(
            [
                lax.dynamic_index_in_dim(parts, row_pos, 0, keepdims=False),
                lax.dynamic_index_in_dim(parts, 1 - row_pos, 0, keepdims=False),
            ]
        )

    x_own = enter(inputs)
    qkv_own = fetch_qkv(w_qkv.astype(LOW), (x_own,))
    out_rows = fetch_out(w_out.astype(LOW))
    gu_sent = send_gate_up(w_gate_up)
    down_sent = send_down(w_down)
    begun = gather_begin(x_own)
    begun = tuple(after(share, gu_sent, down_sent) for share in begun)
    every_place = after(jnp.concatenate([positions, block_map], axis=1), *begun)
    if is_relative() and span == 1:
        twin = other_row(every_place)
        first = row_pos == 0
        every_place = jnp.concatenate(
            [jnp.where(first, every_place, twin), jnp.where(first, twin, every_place)]
        )
        every_place = lax.dynamic_slice_in_dim(every_place, col_pos, 1, 0)
        here = jnp.concatenate(trade_dp([every_place] * n_dp))
        sequences = n_dp
    else:
        every_place = lax.all_gather(every_place, ("dp", "row"), axis=0, tiled=True)
        sequences = n_dp // span
        numbers = []
        for k in range(sequences):
            first = place_of(k) if span == 1 else k * span + col_pos % span
            numbers.append(first * (n_col // span) + col_pos // span)
        here = jnp.concatenate(
            [lax.dynamic_slice_in_dim(every_place, number, 1, 0) for number in numbers]
        )
    places = here[:, :length]
    starts = here[:, length:]
    documents = jnp.cumsum((places == 0).astype(jnp.int32), axis=1)
    x_parts = gather_end(x_own, begun)
    qkv_own = after(qkv_own, *begun)
    qkv_other = other_row(qkv_own)
    x_all = jnp.stack(x_parts)
    gu_own, gu_got = fetch_gate_up(after(gu_sent, x_all), w_gate_up.shape)
    down_own, down_got = fetch_down(after(down_sent, x_all), w_down.shape)
    grad_result = enter(cotangent).astype(FULL)

    token_places = lax.dynamic_index_in_dim(
        places.reshape(n_dp, 2, tokens), row_pos, 1, keepdims=False
    )
    cosine, sine_term = angles(token_places)

    if heads_line_up():
        gain_here = lax.dynamic_index_in_dim(
            gains[:2].reshape(2, n_col, n_dp, HD), data_pos, 2, keepdims=False
        ).reshape(2, local)
    else:
        gain_here = lax.dynamic_slice_in_dim(gains[:2], data_pos * local, local, 1)

    raw, squares = qkv_forward(x_all, qkv_own, qkv_other)
    squares = sum_dp(squares)
    turn = (raw, squares, cosine, sine_term, gain_here)
    out_begun = ()
    if heads_line_up():
        out_begun = gather_begin(after(out_rows, gu_got, down_got))
    packed = rope_forward(*turn, (gu_got, down_got))

    def by_sequence(values):
        if span == 1:
            return values
        last = values.shape[-1]
        values = values.reshape(2, sequences, span, tokens, last).transpose(1, 2, 0, 3, 4)
        return values.reshape(1, sequences, length, last)

    def by_shard(values):
        if span == 1:
            return values
        last = values.shape[-1]
        values = values.reshape(sequences, span, 2, tokens, last).transpose(2, 0, 1, 3, 4)
        return values.reshape(2, n_dp, tokens, last)

    packed = by_sequence(exchange_row(packed))
    out_own = out_rows
    mixed, log_total = attend_forward(packed, starts, documents)
    if heads_line_up():
        out_begun = tuple(after(share, log_total) for share in out_begun)
        out_own = jnp.concatenate(gather_end(out_rows, out_begun), axis=0)
    out_other = other_row(out_own)
    mixed = exchange_row(by_shard(mixed))
    mixed = trade_dp([mixed[:, k] for k in range(n_dp)])
    attended = jnp.concatenate([piece[core] for piece in mixed for core in range(2)], axis=1)

    attn = down_forward(attended, out_own, out_other, FULL, (gu_own,))
    gain_attn = own_first(gains[2])[None, :]
    gain_mlp = own_first(gains[3])[None, :]
    attn_scale = lax.rsqrt(jnp.mean(attn * attn, axis=1, keepdims=True) + EPSILON)
    attn_hat = attn * attn_scale
    hidden_in = x_own.astype(FULL) + attn_hat * gain_attn
    h_own = hidden_in.astype(LOW)
    begun = gather_begin(h_own)
    gu_own = after(gu_own, h_own)
    gu_other = other_row(gu_own)
    by_arrival = list(range(n_dp))
    by_distance = [3, 1, 2, 0] if is_relative() else by_arrival
    gated = [None] * n_dp
    last, rest = (), by_arrival
    if is_relative():
        gated[0] = gate_forward(h_own, gu_own, gu_other)
        last, rest = (gated[0][0],), by_arrival[1:]
        begun = tuple(after(share, *last) for share in begun)
    h_parts = gather_end(h_own, begun)

    def gate_part(k, deps):
        deps = deps + ((h_parts[3], down_own) if k == 2 else ())
        return gate_forward(h_parts[k], gu_own, gu_other, deps)

    in_turn(rest, gate_part, gated, last)
    hiddens = [entry[0] for entry in gated]
    down_own = after(down_own, hiddens[2])
    down_other = other_row(down_own)
    terms = [None] * n_dp
    in_turn(
        by_distance,
        lambda k, deps: down_forward(hiddens[k], down_own, down_other, LOW, deps),
        terms,
    )
    mlp = scatter_dp(terms)
    mlp_scale = lax.rsqrt(jnp.mean(mlp * mlp, axis=1, keepdims=True) + EPSILON)
    mlp_hat = mlp * mlp_scale
    result = leave(hidden_in + mlp_hat * gain_mlp)

    grad_mlp, gain_mlp_grad = norm_back(grad_result, mlp_hat, mlp_scale, gain_mlp)
    m_own = grad_mlp.astype(LOW)
    weights = (gu_own, gu_other, down_own, down_other)
    backs = [None] * n_dp
    begun = gather_begin(m_own)
    if is_relative():
        m_parts = [m_own]
        last = in_turn(
            [0], lambda k, deps: mlp_backward(m_own, *gated[k][1:], *weights, deps), backs
        )
        begun = tuple(after(share, *last) for share in begun)
        rest = [1, 3, 2]
    else:
        last, rest = (), by_arrival
    m_parts = gather_end(m_own, begun)
    last = in_turn(
        rest,
        lambda k, deps: mlp_backward(m_parts[k], *gated[k][1:], *weights, deps),
        backs,
        last,
    )
    units = hiddens[0].shape[1]
    down_block = (hiddens, units, [m_parts], width, 1)
    gu_block = (
        h_parts,
        width,
        [[entry[0] for entry in backs], [entry[1] for entry in backs]],
        gu_own.shape[3],
        n_col,
    )
    terms = [entry[2] for entry in backs]
    begun = scatter_begin(terms)
    gu_rest = grad_for_other(*gu_block, True, last + begun[:3])
    down_rest = grad_for_other(*down_block, False, (gu_rest[0],) + begun[3:])
    middle = scatter_middle(terms, begun)
    gu_half = grad_for_own(*gu_block, gu_rest, (down_rest[0],) + middle)
    gu_sum = reduce_col(gu_half)
    terms[0] = after(terms[0], gu_half)
    grad_hidden_in = grad_result + scatter_end(terms, begun, middle)

    grad_attn, gain_attn_grad = norm_back(grad_hidden_in, attn_hat, attn_scale, gain_attn)
    grad_attn_low = grad_attn.astype(LOW)
    sent = attended_backward(grad_attn_low, out_own, out_other, n_dp, (gu_half,))
    out_block = ([attended], D, [[grad_attn_low]], width, 1)
    out_rest = grad_for_other(*out_block, False, (sent[0],), 4)
    grad_mixed = by_sequence(exchange_row(jnp.stack(trade_dp(sent), axis=1)))
    grads = attend_backward(packed, starts, documents, log_total, grad_mixed, (out_rest[0],))
    out_half = grad_for_own(*out_block, out_rest, (grads,), 4)
    grads = exchange_row(by_shard(grads))
    inner, gain_pair = rope_inner(*turn, grads)
    gu_got = exchange_dp(send_gate_up_grad(gu_sum, w_gate_up.shape))
    out_begun = ()
    if heads_line_up():
        out_parts = out_half.reshape(n_dp, local, width)
        out_parts = [out_parts[k] for k in range(n_dp)]
        out_begun = scatter_begin(out_parts)
    qkv_low = rope_backward(*turn, grads, sum_dp(inner))
    down_half = grad_for_own(*down_block, down_rest, (gu_sum, qkv_low) + out_begun)
    down_sum = reduce_col(down_half.reshape(n_col, -1, width))
    qkv_block = (
        [x_all.reshape(n_dp * tokens, D)],
        width,
        [[qkv_low.reshape(n_dp * tokens, 3 * local)]],
        3 * HD,
        heads_here,
    )
    out_middle = ()
    if heads_line_up():
        out_middle = scatter_middle(out_parts, out_begun)
    qkv_rest = grad_for_other(*qkv_block, True, (down_half,), 4)
    if heads_line_up():
        out_half = scatter_end(out_parts, out_begun, out_middle).astype(LOW)
        out_half = reduce_col(after(out_half.reshape(n_col, HD, width), gu_sum))
    down_got = exchange_dp(send_down_grad(down_sum, w_down.shape))
    grad_gu = gate_up_grad(gu_got, w_gate_up.shape)
    grad_down = down_got.reshape(w_down.shape).astype(FULL)
    grad_out = settle_out(out_half, w_out.shape)
    terms = [None] * n_dp
    back_order = [3, 1, 0, 2] if is_relative() else by_arrival

    def back_term(k, deps):
        deps = deps + ((grad_gu,) if k == back_order[-1] else ())
        return qkv_backward(qkv_low[k], qkv_own, qkv_other, deps)

    last = in_turn(back_order[:1], back_term, terms, (qkv_rest[0],))
    qkv_half = grad_for_own(*qkv_block, qkv_rest, last + out_middle, 4)
    in_turn(back_order[1:], back_term, terms, (qkv_half,))
    begun = scatter_begin(terms)
    middle = scatter_middle(terms, begun)
    if heads_line_up():
        qkv_sum = reduce_col(after(qkv_half[:, 0], down_sum))
    else:
        qkv_sum = qkv_half
    grad_qkv = settle_qkv(qkv_sum, w_qkv.shape)
    grad_inputs = leave(grad_hidden_in + scatter_end(terms, begun, middle))

    if heads_line_up():
        gain_pair = placed(
            (2, n_col, n_dp, HD), gain_pair.reshape(2, n_col, 1, HD), (0, 0, data_pos, 0)
        )
    else:
        gain_pair = placed((2, D), gain_pair, (0, data_pos * local))
    gain_partial = jnp.concatenate(
        [
            gain_pair.reshape(2, D),
            own_first(gain_attn_grad)[None, :],
            own_first(gain_mlp_grad)[None, :],
        ]
    )

    nb_rows, inner_rows, _, heads_col, _ = grad_qkv.shape
    ff_blocks = grad_down.shape[0]
    ff_cols = grad_gu.shape[3]
    row_at = (row_pos * nb_rows, data_pos * inner_rows)
    out_at = (col_pos * heads_col, data_pos * inner_rows)
    down_at = (col_pos * ff_blocks, data_pos * inner_rows)
    own_half = (row_pos * width,)
    rate, down_rate = 3.0 * D ** (-0.5), 3.0 * FF ** (-0.5)
    matrices = [
        (grad_qkv, w_qkv, (D // HD, HD), (3, H, HD), row_at, (0, col_pos * heads_col, 0), rate),
        (grad_out, w_out, (H, HD), (D,), out_at, own_half, rate),
        (grad_gu, w_gate_up, (D // HD, HD), (2, FF), row_at, (0, col_pos * ff_cols), rate),
        (grad_down, w_down, (FF // HD, HD), (D,), down_at, own_half, down_rate),
    ]
    row_part, col_part = square_sums(matrices)
    sums = sum_all(jnp.concatenate([row_part, col_part, gain_partial.reshape(-1)]))
    row_end, col_end = row_part.size, row_part.size + col_part.size
    new_row, new_col = new_states(
        matrices, sums[:row_end], sums[row_end:col_end], row_state, col_state
    )
    gain_grad = sums[col_end:].reshape(gain_partial.shape)
    updates, sizes = scaled_updates(matrices, new_row, new_col)
    new_qkv, new_out, new_gu, new_down = renew(matrices, updates, sum_all(sizes))
    gain_new_state = DECAY * gain_state + (1.0 - DECAY) * (gain_grad * gain_grad + TINY_SQUARE)
    gain_update = gain_grad * lax.rsqrt(gain_new_state)
    gain_update = gain_update / jnp.maximum(
        1.0, jnp.sqrt(jnp.mean(gain_update * gain_update, axis=1, keepdims=True)) / CLIP_LEVEL
    )
    new_gains = gains - GAIN_RATE * gain_update
    return (
        result,
        grad_inputs,
        grad_qkv,
        grad_out,
        grad_gu,
        grad_down,
        new_qkv,
        new_out,
        new_gu,
        new_down,
        new_qkv.astype(LOW),
        new_out.astype(LOW),
        new_gu.astype(LOW),
        new_down.astype(LOW),
        new_row,
        new_col,
        gain_grad,
        gain_new_state,
        new_gains,
    )


def solution(mesh):
    return jax.shard_map(
        shards,
        mesh=mesh,
        in_specs=(
            P(("dp", "col"), "row"),
            P(("dp", "col"), "row"),
            P("row", "dp", None, "col", None),
            P("col", "dp", "row"),
            P("row", "dp", None, "col"),
            P("col", "dp", "row"),
            P(),
            P(),
            P(),
            P(),
            P(("dp", "row"), None),
            P(("dp", "row"), None),
        ),
        out_specs=(
            P(("dp", "col"), "row"),
            P(("dp", "col"), "row"),
            P("row", "dp", None, "col", None),
            P("col", "dp", "row"),
            P("row", "dp", None, "col"),
            P("col", "dp", "row"),
            P("row", "dp", None, "col", None),
            P("col", "dp", "row"),
            P("row", "dp", None, "col"),
            P("col", "dp", "row"),
            P("row", "dp", None, "col", None),
            P("col", "dp", "row"),
            P("row", "dp", None, "col"),
            P("col", "dp", "row"),
            P(),
            P(),
            P(),
            P(),
            P(),
        ),
        check_vma=False,
    )
```

profile of v0, /device:TPU:0, one launch (start us, length us, event | category | flops | bytes accessed | tf_op | source)
XLA Modules:
  0.0 1239.9 jit_solution(5681496922150425117)
XLA Ops:
  60.3 21.9 %collective-permute-done.2.refs_0_ = bf16[512,2048]{1,0:T(8,128)(2,1)} collective-permute-done((bf16[512,2048]{1,0:T(8,128)(2,1)}, bf16[512,2048]{1,0:T(8,128)(2,1)}, u32[]{:S(2)}, u32[]{:S(2)}) %collective-permute-start.2) | collective-permute-done | bytes 2097184 | tf_op jit(solution)/shard_map/ppermute | solution.py:535
  151.2 29.6 %qkv.1 = (f32[4,512,1536]{2,1,0:T(8,128)}, f32[4,2,512]{2,1,0:T(2,128)}) custom-call(bf16[4,512,2048]{2,1,0:T(8,128)(2,1)} %pad_maximum_fusion.x.refs_1_, bf16[4,1024,384]{2,1,0:T(8,128)(2,1)} %after.23.w_own.refs_1_, bf16[4,1024,384]{2,1,0:T(8,128)(2,1)} %collective-permute-done.12.w_other.refs_2_), custom_call_target="tpu_custom_call" | custom-call | flops 25769803776 | bytes 92274688 | tf_op jit(solution)/shard_map/qkv/pallas_call | solution.py:340
  217.2 20.5 %attend.1 = (bf16[2,4,512,256]{3,2,1,0:T(8,128)(2,1)S(1)}, f32[4,2,1,1024]{3,2,1,0:T(1,128)S(1)}) custom-call(s32[4,4]{1,0:T(4,128)S(1)} %pad_add_fusion.4.starts.refs_0_, bf16[2,4,512,768]{3,2,1,0:T(8,128)(2,1)} %constant_dynamic-update-slice_fusion.17.query.key.value.refs_1_.refs_2_.refs_3_, ...), custom_call_target="tpu_custom_call" | custom-call | flops 5368709120 | bytes 25165824 | tf_op jit(solution)/shard_map/attend/pallas_call | solution.py:775
  284.1 11.4 collective-permute-done.24
  330.2 14.9 %gate_up.4 = (bf16[512,2048]{1,0:T(8,128)(2,1)}, bf16[512,2048]{1,0:T(8,128)(2,1)}, bf16[512,2048]{1,0:T(8,128)(2,1)}) custom-call(bf16[512,2048]{1,0:T(8,128)(2,1)} %fusion.7.refs_1_.refs_0_, bf16[4,2,1024,512]{3,2,1,0:T(8,128)(2,1)} %after.29.refs_1_.refs_3_, bf16[4,2,1024,512]{3,2,1,0:T(8,128)(2,1)} %collective-permute-done.34.refs_2_.refs_4_), custom_call_target="tpu_custom_call" | custom-call | flops 17179869184 | bytes 50331648 | tf_op jit(solution)/shard_map/gate_up/pallas_call | solution.py:100
  345.1 20.1 %collective-permute-done.36.refs_0_ = bf16[512,2048]{1,0:T(8,128)(2,1)} collective-permute-done((bf16[512,2048]{1,0:T(8,128)(2,1)}, bf16[512,2048]{1,0:T(8,128)(2,1)}, u32[]{:S(2)}, u32[]{:S(2)}) %collective-permute-start.36) | collective-permute-done | bytes 2097184 | tf_op jit(solution)/shard_map/ppermute | solution.py:535
  371.9 14.7 %gate_up.5 = (bf16[512,2048]{1,0:T(8,128)(2,1)}, bf16[512,2048]{1,0:T(8,128)(2,1)}, bf16[512,2048]{1,0:T(8,128)(2,1)}) custom-call(bf16[512,2048]{1,0:T(8,128)(2,1)} %after.31.refs_0_.refs_1_, bf16[4,2,1024,512]{3,2,1,0:T(8,128)(2,1)} %after.29.refs_1_.refs_3_, bf16[4,2,1024,512]{3,2,1,0:T(8,128)(2,1)} %collective-permute-done.34.refs_2_.refs_4_, ...), custom_call_target="tpu_custom_call" | custom-call | flops 17179869184 | bytes 50331648 | tf_op jit(solution)/shard_map/gate_up/pallas_call | solution.py:100
  397.1 14.6 %gate_up.6 = (bf16[512,2048]{1,0:T(8,128)(2,1)}, bf16[512,2048]{1,0:T(8,128)(2,1)}, bf16[512,2048]{1,0:T(8,128)(2,1)}) custom-call(bf16[512,2048]{1,0:T(8,128)(2,1)} %after.30.refs_0_.refs_2_, bf16[4,2,1024,512]{3,2,1,0:T(8,128)(2,1)} %after.29.refs_1_.refs_3_, bf16[4,2,1024,512]{3,2,1,0:T(8,128)(2,1)} %collective-permute-done.34.refs_2_.refs_4_, ...), custom_call_target="tpu_custom_call" | custom-call | flops 17179869184 | bytes 50331648 | tf_op jit(solution)/shard_map/gate_up/pallas_call | solution.py:100
  411.7 14.7 %gate_up.7 = (bf16[512,2048]{1,0:T(8,128)(2,1)}, bf16[512,2048]{1,0:T(8,128)(2,1)}, bf16[512,2048]{1,0:T(8,128)(2,1)}) custom-call(bf16[512,2048]{1,0:T(8,128)(2,1)} %constant_dynamic-update-slice_fusion.5.refs_4_.refs_0_.refs_3_, bf16[4,2,1024,512]{3,2,1,0:T(8,128)(2,1)} %after.29.refs_1_.refs_3_, ...), custom_call_target="tpu_custom_call" | custom-call | flops 17179869184 | bytes 50331648 | tf_op jit(solution)/shard_map/gate_up/pallas_call | solution.py:100
  493.5 21.1 %collective-permute-done.44 = bf16[256,2048]{1,0:T(8,128)(2,1)} collective-permute-done((bf16[256,2048]{1,0:T(8,128)(2,1)}, bf16[256,2048]{1,0:T(8,128)(2,1)}, u32[]{:S(2)}, u32[]{:S(2)}) %collective-permute-start.44) | collective-permute-done | bytes 1048608 | tf_op jit(solution)/shard_map/ppermute | solution.py:535
  527.3 22.3 %mlp_back.4 = (bf16[512,2048]{1,0:T(8,128)(2,1)}, bf16[512,2048]{1,0:T(8,128)(2,1)}, bf16[512,2048]{1,0:T(8,128)(2,1)}) custom-call(bf16[512,2048]{1,0:T(8,128)(2,1)} %fusion.4.refs_0_.refs_4_, bf16[512,2048]{1,0:T(8,128)(2,1)} %get-tuple-element.69.refs_1_, bf16[512,2048]{1,0:T(8,128)(2,1)} %get-tuple-element.70.refs_2_, ...), custom_call_target="tpu_custom_call" | custom-call | flops 25769803776 | bytes 75497472 | tf_op jit(solution)/shard_map/mlp_back/pallas_call | solution.py:220
  549.6 23.3 %collective-permute-done.49.refs_0_ = bf16[512,2048]{1,0:T(8,128)(2,1)} collective-permute-done((bf16[512,2048]{1,0:T(8,128)(2,1)}, bf16[512,2048]{1,0:T(8,128)(2,1)}, u32[]{:S(2)}, u32[]{:S(2)}) %collective-permute-start.49) | collective-permute-done | bytes 2097184 | tf_op jit(solution)/shard_map/ppermute | solution.py:535
  577.7 22.6 %mlp_back.5 = (bf16[512,2048]{1,0:T(8,128)(2,1)}, bf16[512,2048]{1,0:T(8,128)(2,1)}, bf16[512,2048]{1,0:T(8,128)(2,1)}) custom-call(bf16[512,2048]{1,0:T(8,128)(2,1)} %after.33.refs_0_.refs_5_, bf16[512,2048]{1,0:T(8,128)(2,1)} %get-tuple-element.73.refs_1_, bf16[512,2048]{1,0:T(8,128)(2,1)} %get-tuple-element.74.refs_2_, ...), custom_call_target="tpu_custom_call" | custom-call | flops 25769803776 | bytes 75497472 | tf_op jit(solution)/shard_map/mlp_back/pallas_call | solution.py:220
  606.9 22.3 %mlp_back.6 = (bf16[512,2048]{1,0:T(8,128)(2,1)}, bf16[512,2048]{1,0:T(8,128)(2,1)}, bf16[512,2048]{1,0:T(8,128)(2,1)}) custom-call(bf16[512,2048]{1,0:T(8,128)(2,1)} %copy-done.79, bf16[512,2048]{1,0:T(8,128)(2,1)} %get-tuple-element.78.refs_1_, bf16[512,2048]{1,0:T(8,128)(2,1)} %get-tuple-element.79.refs_2_, ...), custom_call_target="tpu_custom_call" | custom-call | flops 25769803776 | bytes 75497472 | tf_op jit(solution)/shard_map/mlp_back/pallas_call | solution.py:220
  633.9 22.3 %mlp_back.7 = (bf16[512,2048]{1,0:T(8,128)(2,1)}, bf16[512,2048]{1,0:T(8,128)(2,1)}, bf16[512,2048]{1,0:T(8,128)(2,1)}) custom-call(bf16[512,2048]{1,0:T(8,128)(2,1)} %after.34.refs_0_.refs_6_, bf16[512,2048]{1,0:T(8,128)(2,1)} %get-tuple-element.76.refs_1_, bf16[512,2048]{1,0:T(8,128)(2,1)} %get-tuple-element.77.refs_2_, ...), custom_call_target="tpu_custom_call" | custom-call | flops 25769803776 | bytes 75497472 | tf_op jit(solution)/shard_map/mlp_back/pallas_call | solution.py:220
  663.3 28.2 %weight_grad.8 = (bf16[1,2,1024,512]{3,2,1,0:T(8,128)(2,1)}, bf16[1,2,1024,512]{3,2,1,0:T(8,128)(2,1)}, bf16[1,2,1024,512]{3,2,1,0:T(8,128)(2,1)}, bf16[1,2,1024,512]{3,2,1,0:T(8,128)(2,1)}) custom-call(bf16[512,2048]{1,0:T(8,128)(2,1)} %fusion.7.refs_1_.refs_0_, bf16[512,2048]{1,0:T(8,128)(2,1)} %after.31.refs_0_.refs_1_, ...), custom_call_target="tpu_custom_call" | custom-call | flops 34359738368 | bytes 109051904 | tf_op jit(solution)/shard_map/weight_grad/pallas_call | solution.py:291
  704.3 13.5 %weight_grad.9.refs_16_ = bf16[1,1,2048,1024]{3,2,1,0:T(8,128)(2,1)} custom-call(bf16[512,2048]{1,0:T(8,128)(2,1)} %get-tuple-element.65.refs_1_.refs_3_.refs_0_, bf16[512,2048]{1,0:T(8,128)(2,1)} %get-tuple-element.66.refs_3_.refs_0_.refs_1_, bf16[512,2048]{1,0:T(8,128)(2,1)} %get-tuple-element.67.refs_1_.refs_3_.refs_0_.refs_2_, ...), custom_call_target="tpu_custom_call" | custom-call | flops 17179869184 | bytes 67108864 | tf_op jit(solution)/shard_map/weight_grad/pallas_call | solution.py:291
  724.4 30.6 %weight_grad.10.refs_1_.refs_3_ = bf16[4,2,1024,512]{3,2,1,0:T(8,128)(2,1)} custom-call(bf16[512,2048]{1,0:T(8,128)(2,1)} %fusion.7.refs_1_.refs_0_, bf16[512,2048]{1,0:T(8,128)(2,1)} %after.31.refs_0_.refs_1_, bf16[512,2048]{1,0:T(8,128)(2,1)} %after.30.refs_0_.refs_2_, bf16[512,2048]{1,0:T(8,128)(2,1)} %constant_dynamic-update-slice_fusion.5.refs_4_.refs_0_.refs_3_, ...), custom_call_target="tpu_custom_call" | custom-call | flops 34359738368 | bytes 109051904 | tf_op jit(solution)/shard_map/weight_grad/pallas_call | solution.py:291
  813.1 25.2 %attend_back.1.refs_3_ = bf16[2,4,512,768]{3,2,1,0:T(8,128)(2,1)} custom-call(s32[4,4]{1,0:T(4,128)S(1)} %copy-done.5, bf16[2,4,512,768]{3,2,1,0:T(8,128)(2,1)} %constant_dynamic-update-slice_fusion.17.query.key.value.refs_1_.refs_2_.refs_3_, bf16[2,4,512,768]{3,2,1,0:T(8,128)(2,1)} %constant_dynamic-update-slice_fusion.17.query.key.value.refs_1_.refs_2_.refs_3_, ...), custom_call_target="tpu_custom_call" | custom-call | flops 33554432000 | bytes 62914560 | tf_op jit(solution)/shard_map/attend_back/pallas_call | solution.py:806
  876.8 12.3 rope_back.1.refs_10_
  897.9 14.0 %weight_grad.13.refs_2_ = bf16[1,1,2048,1024]{3,2,1,0:T(8,128)(2,1)} custom-call(bf16[512,2048]{1,0:T(8,128)(2,1)} %get-tuple-element.65.refs_1_.refs_3_.refs_0_, bf16[512,2048]{1,0:T(8,128)(2,1)} %get-tuple-element.66.refs_3_.refs_0_.refs_1_, bf16[512,2048]{1,0:T(8,128)(2,1)} %get-tuple-element.67.refs_1_.refs_3_.refs_0_.refs_2_, ...), custom_call_target="tpu_custom_call" | custom-call | flops 17179869184 | bytes 67108864 | tf_op jit(solution)/shard_map/weight_grad/pallas_call | solution.py:291
  937.0 16.2 %weight_grad.14 = (bf16[1,1,1024,384]{3,2,1,0:T(8,128)(2,1)}, bf16[1,1,1024,384]{3,2,1,0:T(8,128)(2,1)}, bf16[1,1,1024,384]{3,2,1,0:T(8,128)(2,1)}, bf16[1,1,1024,384]{3,2,1,0:T(8,128)(2,1)}) custom-call(bf16[2048,2048]{1,0:T(8,128)(2,1)} %bitcast.407, bf16[2048,1536]{1,0:T(8,128)(2,1)} %bitcast.421, bf16[1,1,2048,1024]{3,2,1,0:T(8,128)(2,1)} %weight_grad.13.refs_2_), custom_call_target="tpu_custom_call" | custom-call | flops 25769803776 | bytes 92274688 | tf_op jit(solution)/shard_map/weight_grad/pallas_call | solution.py:291
  984.1 17.3 %weight_grad.15.refs_3_ = bf16[4,1,1024,384]{3,2,1,0:T(8,128)(2,1)} custom-call(bf16[2048,2048]{1,0:T(8,128)(2,1)} %bitcast.408, bf16[2048,1536]{1,0:T(8,128)(2,1)} %bitcast.422, bf16[1,1,1024,384]{3,2,1,0:T(8,128)(2,1)} %collective-permute-done.75.refs_2_, bf16[1,1,1024,384]{3,2,1,0:T(8,128)(2,1)} %collective-permute-done.76.refs_3_, ...), custom_call_target="tpu_custom_call" | custom-call | flops 25769803776 | bytes 92274688 | tf_op jit(solution)/shard_map/weight_grad/pallas_call | solution.py:291
  1060.3 19.3 %collective-permute-done.88 = bf16[256,2048]{1,0:T(8,128)(2,1)} collective-permute-done((bf16[256,2048]{1,0:T(8,128)(2,1)}, bf16[256,2048]{1,0:T(8,128)(2,1)}, u32[]{:S(2)}, u32[]{:S(2)}) %collective-permute-start.88) | collective-permute-done | bytes 1048608 | tf_op jit(solution)/shard_map/ppermute | solution.py:535
  (794 shorter events, 745.0 us)
Async XLA Ops:
  7.2 91.4 %all-gather.5.cloned.1.call-start = ((), (), s32[]{:S(2)}) async-start(), calls=%async_computation.4 | async-start | bytes 3932160 | tf_op jit(solution)/shard_map/all_gather | solution.py:892
  33.5 171.8 %all-gather.7.cloned.1.call-start = ((), (), s32[]{:S(2)}) async-start(), calls=%async_computation.5 | async-start | bytes 1310720 | tf_op jit(solution)/shard_map/all_gather | solution.py:901
  33.5 48.6 %collective-permute-start.2 = (bf16[512,2048]{1,0:T(8,128)(2,1)}, bf16[512,2048]{1,0:T(8,128)(2,1)}, u32[]{:S(2)}, u32[]{:S(2)}) collective-permute-start(bf16[512,2048]{1,0:T(8,128)(2,1)} %get-tuple-element.260.refs_1_), channel_id=1, source_target_pairs={{0,16},{8,24},{16,0},{24,8},{1,17},{9,25},{17,1},{25,9},{2,18},{10... | collective-permute-start | bytes 6291464 | tf_op jit(solution)/shard_map/ppermute | solution.py:535
  35.3 50.5 %collective-permute-start.1 = (bf16[512,2048]{1,0:T(8,128)(2,1)}, bf16[512,2048]{1,0:T(8,128)(2,1)S(1)}, u32[]{:S(2)}, u32[]{:S(2)}) collective-permute-start(bf16[512,2048]{1,0:T(8,128)(2,1)} %get-tuple-element.260.refs_1_), channel_id=1, source_target_pairs={{0,8},{8,0},{16,24},{24,16},{1,9},{9,1},{17,25},{25,17},{2,10},{10... | collective-permute-start | bytes 6291464 | tf_op jit(solution)/shard_map/ppermute | solution.py:535
  38.5 60.0 %collective-permute-start.26 = (bf16[32,1024]{1,0:T(8,128)(2,1)}, bf16[32,1024]{1,0:T(8,128)(2,1)S(1)}, u32[]{:S(2)}, u32[]{:S(2)}) collective-permute-start(bf16[32,1024]{1,0:T(8,128)(2,1)} %get-tuple-element.304), channel_id=1, source_target_pairs={{0,24},{8,16},{16,8},{24,0},{1,25},{9,17},{17,9},{25,1},{2,26},{10... | collective-permute-start | bytes 196616 | tf_op jit(solution)/shard_map/ppermute | solution.py:535
  38.9 59.7 %collective-permute-start.27 = (bf16[32,1024]{1,0:T(8,128)(2,1)}, bf16[32,1024]{1,0:T(8,128)(2,1)S(1)}, u32[]{:S(2)}, u32[]{:S(2)}) collective-permute-start(bf16[32,1024]{1,0:T(8,128)(2,1)} %get-tuple-element.303), channel_id=1, source_target_pairs={{0,16},{8,24},{16,0},{24,8},{1,17},{9,25},{17,1},{25,9},{2,18},{10... | collective-permute-start | bytes 196616 | tf_op jit(solution)/shard_map/ppermute | solution.py:535
  40.5 59.3 %collective-permute-start.28 = (bf16[32,1024]{1,0:T(8,128)(2,1)}, bf16[32,1024]{1,0:T(8,128)(2,1)}, u32[]{:S(2)}, u32[]{:S(2)}) collective-permute-start(bf16[32,1024]{1,0:T(8,128)(2,1)} %get-tuple-element.302), channel_id=1, source_target_pairs={{0,8},{8,0},{16,24},{24,16},{1,9},{9,1},{17,25},{25,17},{2,10},{10... | collective-permute-start | bytes 196616 | tf_op jit(solution)/shard_map/ppermute | solution.py:535
  98.6 52.6 %collective-permute-start.12 = (bf16[4,1024,384]{2,1,0:T(8,128)(2,1)}, bf16[4,1024,384]{2,1,0:T(8,128)(2,1)}, u32[]{:S(2)}, u32[]{:S(2)}) collective-permute-start(bf16[4,1024,384]{2,1,0:T(8,128)(2,1)} %after.23.w_own.refs_1_), channel_id=1, source_target_pairs={{0,4},{4,0},{1,5},{5,1},{2,6},{6,2},{3,7},{7,3},{8,12},{12,8},{9,1... | collective-permute-start | bytes 9437192 | tf_op jit(solution)/shard_map/ppermute | solution.py:535
  103.0 198.4 %all-gather.9.cloned.1.call-start = ((), (), s32[]{:S(2)}) async-start(), calls=%async_computation.6 | async-start | bytes 10485760 | tf_op jit(solution)/shard_map/all_gather | solution.py:919
  130.6 51.2 %collective-permute-start.18 = (bf16[128,1024]{1,0:T(8,128)(2,1)}, bf16[128,1024]{1,0:T(8,128)(2,1)S(1)}, u32[]{:S(2)}, u32[]{:S(2)}) collective-permute-start(bf16[128,1024]{1,0:T(8,128)(2,1)} %get-tuple-element.284), channel_id=1, source_target_pairs={{0,24},{8,16},{16,8},{24,0},{1,25},{9,17},{17,9},{25,1},{2,26},{10... | collective-permute-start | bytes 786440 | tf_op jit(solution)/shard_map/ppermute | solution.py:535
  150.7 246.4 %all-gather.11.cloned.1.call-start = ((), (), s32[]{:S(2)}) async-start(), calls=%async_computation.7 | async-start | bytes 5242880 | tf_op jit(solution)/shard_map/all_gather | solution.py:934
  316.8 580.4 %reduce-scatter.5.cloned.1.call-start = ((), (), s32[]{:S(2)}) async-start(), calls=%async_computation.8 | async-start | bytes 10485760 | tf_op jit(solution)/shard_map/reduce_scatter | solution.py:938
  316.9 48.4 %collective-permute-start.36 = (bf16[512,2048]{1,0:T(8,128)(2,1)}, bf16[512,2048]{1,0:T(8,128)(2,1)}, u32[]{:S(2)}, u32[]{:S(2)}) collective-permute-start(bf16[512,2048]{1,0:T(8,128)(2,1)} %fusion.7.refs_1_.refs_0_), channel_id=1, source_target_pairs={{0,8},{8,0},{16,24},{24,16},{1,9},{9,1},{17,25},{25,17},{2,10},{10... | collective-permute-start | bytes 6291464 | tf_op jit(solution)/shard_map/ppermute | solution.py:535
  318.4 50.6 %collective-permute-start.35 = (bf16[512,2048]{1,0:T(8,128)(2,1)}, bf16[512,2048]{1,0:T(8,128)(2,1)}, u32[]{:S(2)}, u32[]{:S(2)}) collective-permute-start(bf16[512,2048]{1,0:T(8,128)(2,1)} %fusion.7.refs_1_.refs_0_), channel_id=1, source_target_pairs={{0,16},{8,24},{16,0},{24,8},{1,17},{9,25},{17,1},{25,9},{2,18},{10... | collective-permute-start | bytes 6291464 | tf_op jit(solution)/shard_map/ppermute | solution.py:535
  526.2 46.6 %collective-permute-start.49 = (bf16[512,2048]{1,0:T(8,128)(2,1)}, bf16[512,2048]{1,0:T(8,128)(2,1)}, u32[]{:S(2)}, u32[]{:S(2)}) collective-permute-start(bf16[512,2048]{1,0:T(8,128)(2,1)} %fusion.4.refs_0_.refs_4_), channel_id=1, source_target_pairs={{0,16},{8,24},{16,0},{24,8},{1,17},{9,25},{17,1},{25,9},{2,18},{10... | collective-permute-start | bytes 6291464 | tf_op jit(solution)/shard_map/ppermute | solution.py:535
  526.8 48.9 %collective-permute-start.48 = (bf16[512,2048]{1,0:T(8,128)(2,1)}, bf16[512,2048]{1,0:T(8,128)(2,1)}, u32[]{:S(2)}, u32[]{:S(2)}) collective-permute-start(bf16[512,2048]{1,0:T(8,128)(2,1)} %fusion.4.refs_0_.refs_4_), channel_id=1, source_target_pairs={{0,8},{8,0},{16,24},{24,16},{1,9},{9,1},{17,25},{25,17},{2,10},{10... | collective-permute-start | bytes 6291464 | tf_op jit(solution)/shard_map/ppermute | solution.py:535
  602.6 59.4 %collective-permute-start.54 = (bf16[256,2048]{1,0:T(8,128)(2,1)}, bf16[256,2048]{1,0:T(8,128)(2,1)S(1)}, u32[]{:S(2)}, u32[]{:S(2)}) collective-permute-start(bf16[256,2048]{1,0:T(8,128)(2,1)} %slice.432), channel_id=1, source_target_pairs={{0,8},{8,0},{16,24},{24,16},{1,9},{9,1},{17,25},{25,17},{2,10},{10... | collective-permute-start | bytes 3145736 | tf_op jit(solution)/shard_map/ppermute | solution.py:535
  755.1 255.1 %reduce-scatter.7.cloned.1.call-start = ((), (), s32[]{:S(2)}) async-start(), calls=%async_computation.9 | async-start | bytes 5242880 | tf_op jit(solution)/shard_map/reduce_scatter | solution.py:938
  912.0 139.0 %reduce-scatter.11.cloned.1.call-start = ((), (), s32[]{:S(2)}) async-start(), calls=%async_computation.11 | async-start | bytes 1310720 | tf_op jit(solution)/shard_map/reduce_scatter | solution.py:938
  966.3 134.0 %reduce-scatter.9.cloned.1.call-start = ((), (), s32[]{:S(2)}) async-start(), calls=%async_computation.10 | async-start | bytes 3932160 | tf_op jit(solution)/shard_map/reduce_scatter | solution.py:938
  967.2 66.1 %collective-permute-start.87 = (bf16[256,2048]{1,0:T(8,128)(2,1)}, bf16[256,2048]{1,0:T(8,128)(2,1)}, u32[]{:S(2)}, u32[]{:S(2)}) collective-permute-start(bf16[256,2048]{1,0:T(8,128)(2,1)} %get-tuple-element.243), channel_id=1, source_target_pairs={{0,16},{8,24},{16,0},{24,8},{1,17},{9,25},{17,1},{25,9},{2,18},{10... | collective-permute-start | bytes 3145736 | tf_op jit(solution)/shard_map/ppermute | solution.py:535
  983.5 52.9 %collective-permute-start.85 = (bf16[256,2048]{1,0:T(8,128)(2,1)}, bf16[256,2048]{1,0:T(8,128)(2,1)S(1)}, u32[]{:S(2)}, u32[]{:S(2)}) collective-permute-start(bf16[256,2048]{1,0:T(8,128)(2,1)} %get-tuple-element.242), channel_id=1, source_target_pairs={{0,8},{8,0},{16,24},{24,16},{1,9},{9,1},{17,25},{25,17},{2,10},{10... | collective-permute-start | bytes 3145736 | tf_op jit(solution)/shard_map/ppermute | solution.py:535
  1045.1 112.5 %collective-permute-start.46 = (f32[512,1024]{1,0:T(8,128)}, f32[512,1024]{1,0:T(8,128)}, u32[]{:S(2)}, u32[]{:S(2)}) collective-permute-start(f32[512,1024]{1,0:T(8,128)} %get-tuple-element.228), channel_id=1, source_target_pairs={{0,4},{4,0},{1,5},{5,1},{2,6},{6,2},{3,7},{7,3},{8,12},{12,8},{9,1... | collective-permute-start | bytes 6291464 | tf_op jit(solution)/shard_map/ppermute | solution.py:535
  1092.7 68.0 %collective-permute-start.90 = (f32[512,1024]{1,0:T(8,128)}, f32[512,1024]{1,0:T(8,128)}, u32[]{:S(2)}, u32[]{:S(2)}) collective-permute-start(f32[512,1024]{1,0:T(8,128)} %get-tuple-element.216), channel_id=1, source_target_pairs={{0,4},{4,0},{1,5},{5,1},{2,6},{6,2},{3,7},{7,3},{8,12},{12,8},{9,1... | collective-permute-start | bytes 6291464 | tf_op jit(solution)/shard_map/ppermute | solution.py:535
  (230 other events, 3146.4 us)
Sparse Core Ops, SparseCore 0:
  33.6 64.8 all-gather.4
  103.2 26.5 all-gather.6
  150.8 150.5 all-gather.8
  316.9 79.0 all-gather.10
  755.2 141.9 reduce-scatter.4
  912.1 76.8 reduce-scatter.6
  991.3 27.6 reduce-scatter.10
  1021.3 58.8 reduce-scatter.8
where the time goes:
time: 1250 us; the launch traced here: 1240 us
  Pallas kernels  483 us (39%)
  waiting for transfers between devices  294 us (24%)
  local copies, waits for them, and re-layouts  184 us (15%)
  other arithmetic  147 us (12%)
  starting transfers between devices  110 us (9%)
  between operations  22.2 us (2%)
    ppermute x110, waiting for transfers between devices, swap(): return lax.ppermute(values, axis, [(i, i ^ step) for i in range(count)])  282 us
    pallas_call x8, Pallas kernels, grad_block(): pl.pallas_call(with_deps(functools.partial(grad_kernel, count, groups, le...  133 us
    ppermute x110, starting transfers between devices, swap(): return lax.ppermute(values, axis, [(i, i ^ step) for i in range(count)])  109 us
    pallas_call x4, Pallas kernels, mlp_backward(): pl.pallas_call(with_deps(mlp_back_kernel, 7, deps), grid=(n_col,), in_spe...  89.4 us
    pallas_call x4, Pallas kernels, gate_forward(): pl.pallas_call(with_deps(gate_kernel, 3, deps), grid=(n_col,), in_specs=[...  58.9 us
    unnamed x296, local copies, waits for them, and re-layouts  51.2 us
    pallas_call x5, Pallas kernels, down_forward(): pl.pallas_call(with_deps(down_kernel, 3, deps), grid=(tokens // rows,), i...  48.1 us
    pallas_call x4, Pallas kernels, qkv_backward(): pl.pallas_call(with_deps(qkv_back_kernel, 3, deps), grid=(tokens // rows,...  35.5 us
  transfers between devices with their start and end apart: 118, of which 49 were waited for; matrix products, arithmetic and copies ran while one was open for 19% of the time, Pallas kernels for 33%

commit v1 on v0

--- a/solution.py
+++ b/solution.py
@@ -938,6 +938,17 @@
     return lax.psum_scatter(values, "col", scatter_dimension=0)
 
 
+def reduce_col_by_permutes(values):
+    if lax.axis_size("col") != 4:
+        return reduce_col(values)
+    me = lax.axis_index("col")
+    total = lax.dynamic_index_in_dim(values, me, 0, keepdims=False).astype(FULL)
+    for k in range(1, 4):
+        sent = lax.dynamic_index_in_dim(values, me ^ k, 0, keepdims=False)
+        total = total + swap(sent, "col", k).astype(FULL)
+    return total.astype(LOW)
+
+
 def grad_for_other(left, rows, right, columns, steps, by_rows, deps=(), factor=2):
     places = (1, 0) if by_rows else (0, 1)
     return grad_block(left, places[0], rows, right, places[1], columns, steps, (), deps, factor, True)
@@ -1310,7 +1321,7 @@
     qkv_rest = grad_for_other(*qkv_block, True, (down_half,), 4)
     if heads_line_up():
         out_half = scatter_end(out_parts, out_begun, out_middle).astype(LOW)
-        out_half = reduce_col(after(out_half.reshape(n_col, HD, width), gu_sum))
+        out_half = reduce_col_by_permutes(after(out_half.reshape(n_col, HD, width), qkv_rest[0]))
     down_got = exchange_dp(send_down_grad(down_sum, w_down.shape))
     grad_gu = gate_up_grad(gu_got, w_gate_up.shape)
     grad_down = down_got.reshape(w_down.shape).astype(FULL)

time: 1250 us -> 1300 us (1.040)
  waiting for transfers between devices: 294 us -> 313 us
  starting transfers between devices: 110 us -> 125 us
    ppermute x110 -> x113, waiting for transfers between devices: 282 us -> 301 us  [swap(): return lax.ppermute(values, axis, [(i, i ^ step) for i in range(count)])]
    ppermute x110 -> x113, starting transfers between devices: 109 us -> 125 us  [swap(): return lax.ppermute(values, axis, [(i, i ^ step) for i in range(count)])]
    unnamed x296 -> x287, local copies, waits for them, and re-layouts: 51.2 us -> 53 us
  transfers between devices with their start and end apart: 118 -> 120, of which waited for: 49 -> 46; matrix products, arithmetic and copies ran while one was open for 19% -> 19% of each run, Pallas kernels for 33% -> 33%
where the time goes in v1:
time: 1300 us; the launch traced here: 1290 us
  Pallas kernels  483 us (37%)
  waiting for transfers between devices  313 us (24%)
  local copies, waits for them, and re-layouts  194 us (15%)
  other arithmetic  150 us (12%)
  starting transfers between devices  125 us (10%)
  between operations  21.8 us (2%)
    ppermute x113, waiting for transfers between devices, swap(): return lax.ppermute(values, axis, [(i, i ^ step) for i in range(count)])  301 us
    pallas_call x8, Pallas kernels, grad_block(): pl.pallas_call(with_deps(functools.partial(grad_kernel, count, groups, le...  133 us
    ppermute x113, starting transfers between devices, swap(): return lax.ppermute(values, axis, [(i, i ^ step) for i in range(count)])  125 us
    pallas_call x4, Pallas kernels, mlp_backward(): pl.pallas_call(with_deps(mlp_back_kernel, 7, deps), grid=(n_col,), in_spe...  89.5 us
    pallas_call x4, Pallas kernels, gate_forward(): pl.pallas_call(with_deps(gate_kernel, 3, deps), grid=(n_col,), in_specs=[...  58.8 us
    unnamed x287, local copies, waits for them, and re-layouts  53 us
    pallas_call x5, Pallas kernels, down_forward(): pl.pallas_call(with_deps(down_kernel, 3, deps), grid=(tokens // rows,), i...  48 us
    pallas_call x4, Pallas kernels, qkv_backward(): pl.pallas_call(with_deps(qkv_back_kernel, 3, deps), grid=(tokens // rows,...  36 us
  transfers between devices with their start and end apart: 120, of which 46 were waited for; matrix products, arithmetic and copies ran while one was open for 19% of the time, Pallas kernels for 33%

profile of v1, /device:TPU:0, one launch (start us, length us, event | category | flops | bytes accessed | tf_op | source)
XLA Modules:
  0.0 1287.5 jit_solution(15674646212791343658)
XLA Ops:
  60.3 21.9 %collective-permute-done.2.refs_0_ = bf16[512,2048]{1,0:T(8,128)(2,1)} collective-permute-done((bf16[512,2048]{1,0:T(8,128)(2,1)}, bf16[512,2048]{1,0:T(8,128)(2,1)}, u32[]{:S(2)}, u32[]{:S(2)}) %collective-permute-start.2) | collective-permute-done | bytes 2097184 | tf_op jit(solution)/shard_map/ppermute | solution.py:535
  151.2 29.6 %qkv.1 = (f32[4,512,1536]{2,1,0:T(8,128)}, f32[4,2,512]{2,1,0:T(2,128)}) custom-call(bf16[4,512,2048]{2,1,0:T(8,128)(2,1)} %pad_maximum_fusion.x.refs_1_, bf16[4,1024,384]{2,1,0:T(8,128)(2,1)} %after.23.w_own.refs_1_, bf16[4,1024,384]{2,1,0:T(8,128)(2,1)} %collective-permute-done.12.w_other.refs_2_), custom_call_target="tpu_custom_call" | custom-call | flops 25769803776 | bytes 92274688 | tf_op jit(solution)/shard_map/qkv/pallas_call | solution.py:340
  217.2 20.5 %attend.1 = (bf16[2,4,512,256]{3,2,1,0:T(8,128)(2,1)S(1)}, f32[4,2,1,1024]{3,2,1,0:T(1,128)S(1)}) custom-call(s32[4,4]{1,0:T(4,128)S(1)} %pad_add_fusion.4.starts.refs_0_, bf16[2,4,512,768]{3,2,1,0:T(8,128)(2,1)} %constant_dynamic-update-slice_fusion.17.query.key.value.refs_1_.refs_2_.refs_3_, ...), custom_call_target="tpu_custom_call" | custom-call | flops 5368709120 | bytes 25165824 | tf_op jit(solution)/shard_map/attend/pallas_call | solution.py:775
  330.2 14.8 %gate_up.4 = (bf16[512,2048]{1,0:T(8,128)(2,1)}, bf16[512,2048]{1,0:T(8,128)(2,1)}, bf16[512,2048]{1,0:T(8,128)(2,1)}) custom-call(bf16[512,2048]{1,0:T(8,128)(2,1)} %fusion.7.refs_1_.refs_0_, bf16[4,2,1024,512]{3,2,1,0:T(8,128)(2,1)} %after.29.refs_1_.refs_3_, bf16[4,2,1024,512]{3,2,1,0:T(8,128)(2,1)} %collective-permute-done.34.refs_2_.refs_4_), custom_call_target="tpu_custom_call" | custom-call | flops 17179869184 | bytes 50331648 | tf_op jit(solution)/shard_map/gate_up/pallas_call | solution.py:100
  345.1 20.2 %collective-permute-done.36.refs_0_ = bf16[512,2048]{1,0:T(8,128)(2,1)} collective-permute-done((bf16[512,2048]{1,0:T(8,128)(2,1)}, bf16[512,2048]{1,0:T(8,128)(2,1)}, u32[]{:S(2)}, u32[]{:S(2)}) %collective-permute-start.36) | collective-permute-done | bytes 2097184 | tf_op jit(solution)/shard_map/ppermute | solution.py:535
  371.9 14.7 %gate_up.5 = (bf16[512,2048]{1,0:T(8,128)(2,1)}, bf16[512,2048]{1,0:T(8,128)(2,1)}, bf16[512,2048]{1,0:T(8,128)(2,1)}) custom-call(bf16[512,2048]{1,0:T(8,128)(2,1)} %after.31.refs_0_.refs_1_, bf16[4,2,1024,512]{3,2,1,0:T(8,128)(2,1)} %after.29.refs_1_.refs_3_, bf16[4,2,1024,512]{3,2,1,0:T(8,128)(2,1)} %collective-permute-done.34.refs_2_.refs_4_, ...), custom_call_target="tpu_custom_call" | custom-call | flops 17179869184 | bytes 50331648 | tf_op jit(solution)/shard_map/gate_up/pallas_call | solution.py:100
  397.1 14.6 %gate_up.6 = (bf16[512,2048]{1,0:T(8,128)(2,1)}, bf16[512,2048]{1,0:T(8,128)(2,1)}, bf16[512,2048]{1,0:T(8,128)(2,1)}) custom-call(bf16[512,2048]{1,0:T(8,128)(2,1)} %after.30.refs_0_.refs_2_, bf16[4,2,1024,512]{3,2,1,0:T(8,128)(2,1)} %after.29.refs_1_.refs_3_, bf16[4,2,1024,512]{3,2,1,0:T(8,128)(2,1)} %collective-permute-done.34.refs_2_.refs_4_, ...), custom_call_target="tpu_custom_call" | custom-call | flops 17179869184 | bytes 50331648 | tf_op jit(solution)/shard_map/gate_up/pallas_call | solution.py:100
  411.7 14.7 %gate_up.7 = (bf16[512,2048]{1,0:T(8,128)(2,1)}, bf16[512,2048]{1,0:T(8,128)(2,1)}, bf16[512,2048]{1,0:T(8,128)(2,1)}) custom-call(bf16[512,2048]{1,0:T(8,128)(2,1)} %constant_dynamic-update-slice_fusion.5.refs_4_.refs_0_.refs_3_, bf16[4,2,1024,512]{3,2,1,0:T(8,128)(2,1)} %after.29.refs_1_.refs_3_, ...), custom_call_target="tpu_custom_call" | custom-call | flops 17179869184 | bytes 50331648 | tf_op jit(solution)/shard_map/gate_up/pallas_call | solution.py:100
  493.4 21.1 %collective-permute-done.44 = bf16[256,2048]{1,0:T(8,128)(2,1)} collective-permute-done((bf16[256,2048]{1,0:T(8,128)(2,1)}, bf16[256,2048]{1,0:T(8,128)(2,1)}, u32[]{:S(2)}, u32[]{:S(2)}) %collective-permute-start.44) | collective-permute-done | bytes 1048608 | tf_op jit(solution)/shard_map/ppermute | solution.py:535
  527.2 22.3 %mlp_back.4 = (bf16[512,2048]{1,0:T(8,128)(2,1)}, bf16[512,2048]{1,0:T(8,128)(2,1)}, bf16[512,2048]{1,0:T(8,128)(2,1)}) custom-call(bf16[512,2048]{1,0:T(8,128)(2,1)} %fusion.4.refs_0_.refs_4_, bf16[512,2048]{1,0:T(8,128)(2,1)} %get-tuple-element.69.refs_1_, bf16[512,2048]{1,0:T(8,128)(2,1)} %get-tuple-element.70.refs_2_, ...), custom_call_target="tpu_custom_call" | custom-call | flops 25769803776 | bytes 75497472 | tf_op jit(solution)/shard_map/mlp_back/pallas_call | solution.py:220
  549.5 23.2 %collective-permute-done.49.refs_0_ = bf16[512,2048]{1,0:T(8,128)(2,1)} collective-permute-done((bf16[512,2048]{1,0:T(8,128)(2,1)}, bf16[512,2048]{1,0:T(8,128)(2,1)}, u32[]{:S(2)}, u32[]{:S(2)}) %collective-permute-start.49) | collective-permute-done | bytes 2097184 | tf_op jit(solution)/shard_map/ppermute | solution.py:535
  577.6 22.6 %mlp_back.5 = (bf16[512,2048]{1,0:T(8,128)(2,1)}, bf16[512,2048]{1,0:T(8,128)(2,1)}, bf16[512,2048]{1,0:T(8,128)(2,1)}) custom-call(bf16[512,2048]{1,0:T(8,128)(2,1)} %after.33.refs_0_.refs_5_, bf16[512,2048]{1,0:T(8,128)(2,1)} %get-tuple-element.73.refs_1_, bf16[512,2048]{1,0:T(8,128)(2,1)} %get-tuple-element.74.refs_2_, ...), custom_call_target="tpu_custom_call" | custom-call | flops 25769803776 | bytes 75497472 | tf_op jit(solution)/shard_map/mlp_back/pallas_call | solution.py:220
  606.8 22.3 %mlp_back.6 = (bf16[512,2048]{1,0:T(8,128)(2,1)}, bf16[512,2048]{1,0:T(8,128)(2,1)}, bf16[512,2048]{1,0:T(8,128)(2,1)}) custom-call(bf16[512,2048]{1,0:T(8,128)(2,1)} %copy-done.72, bf16[512,2048]{1,0:T(8,128)(2,1)} %get-tuple-element.78.refs_1_, bf16[512,2048]{1,0:T(8,128)(2,1)} %get-tuple-element.79.refs_2_, ...), custom_call_target="tpu_custom_call" | custom-call | flops 25769803776 | bytes 75497472 | tf_op jit(solution)/shard_map/mlp_back/pallas_call | solution.py:220
  633.8 22.3 %mlp_back.7 = (bf16[512,2048]{1,0:T(8,128)(2,1)}, bf16[512,2048]{1,0:T(8,128)(2,1)}, bf16[512,2048]{1,0:T(8,128)(2,1)}) custom-call(bf16[512,2048]{1,0:T(8,128)(2,1)} %after.34.refs_0_.refs_6_, bf16[512,2048]{1,0:T(8,128)(2,1)} %get-tuple-element.76.refs_1_, bf16[512,2048]{1,0:T(8,128)(2,1)} %get-tuple-element.77.refs_2_, ...), custom_call_target="tpu_custom_call" | custom-call | flops 25769803776 | bytes 75497472 | tf_op jit(solution)/shard_map/mlp_back/pallas_call | solution.py:220
  663.3 28.2 %weight_grad.8 = (bf16[1,2,1024,512]{3,2,1,0:T(8,128)(2,1)}, bf16[1,2,1024,512]{3,2,1,0:T(8,128)(2,1)}, bf16[1,2,1024,512]{3,2,1,0:T(8,128)(2,1)}, bf16[1,2,1024,512]{3,2,1,0:T(8,128)(2,1)}) custom-call(bf16[512,2048]{1,0:T(8,128)(2,1)} %fusion.7.refs_1_.refs_0_, bf16[512,2048]{1,0:T(8,128)(2,1)} %after.31.refs_0_.refs_1_, ...), custom_call_target="tpu_custom_call" | custom-call | flops 34359738368 | bytes 109051904 | tf_op jit(solution)/shard_map/weight_grad/pallas_call | solution.py:291
  704.2 13.5 %weight_grad.9.refs_16_ = bf16[1,1,2048,1024]{3,2,1,0:T(8,128)(2,1)} custom-call(bf16[512,2048]{1,0:T(8,128)(2,1)} %get-tuple-element.65.refs_1_.refs_3_.refs_0_, bf16[512,2048]{1,0:T(8,128)(2,1)} %get-tuple-element.66.refs_3_.refs_0_.refs_1_, bf16[512,2048]{1,0:T(8,128)(2,1)} %get-tuple-element.67.refs_1_.refs_3_.refs_0_.refs_2_, ...), custom_call_target="tpu_custom_call" | custom-call | flops 17179869184 | bytes 67108864 | tf_op jit(solution)/shard_map/weight_grad/pallas_call | solution.py:291
  724.5 30.5 %weight_grad.10.refs_1_.refs_3_ = bf16[4,2,1024,512]{3,2,1,0:T(8,128)(2,1)} custom-call(bf16[512,2048]{1,0:T(8,128)(2,1)} %fusion.7.refs_1_.refs_0_, bf16[512,2048]{1,0:T(8,128)(2,1)} %after.31.refs_0_.refs_1_, bf16[512,2048]{1,0:T(8,128)(2,1)} %after.30.refs_0_.refs_2_, bf16[512,2048]{1,0:T(8,128)(2,1)} %constant_dynamic-update-slice_fusion.5.refs_4_.refs_0_.refs_3_, ...), custom_call_target="tpu_custom_call" | custom-call | flops 34359738368 | bytes 109051904 | tf_op jit(solution)/shard_map/weight_grad/pallas_call | solution.py:291
  812.9 25.2 %attend_back.1.refs_3_ = bf16[2,4,512,768]{3,2,1,0:T(8,128)(2,1)} custom-call(s32[4,4]{1,0:T(4,128)S(1)} %copy-done.5, bf16[2,4,512,768]{3,2,1,0:T(8,128)(2,1)} %constant_dynamic-update-slice_fusion.17.query.key.value.refs_1_.refs_2_.refs_3_, bf16[2,4,512,768]{3,2,1,0:T(8,128)(2,1)} %constant_dynamic-update-slice_fusion.17.query.key.value.refs_1_.refs_2_.refs_3_, ...), custom_call_target="tpu_custom_call" | custom-call | flops 33554432000 | bytes 62914560 | tf_op jit(solution)/shard_map/attend_back/pallas_call | solution.py:806
  907.5 14.0 %weight_grad.13.refs_2_ = bf16[1,1,2048,1024]{3,2,1,0:T(8,128)(2,1)} custom-call(bf16[512,2048]{1,0:T(8,128)(2,1)} %get-tuple-element.65.refs_1_.refs_3_.refs_0_, bf16[512,2048]{1,0:T(8,128)(2,1)} %get-tuple-element.66.refs_3_.refs_0_.refs_1_, bf16[512,2048]{1,0:T(8,128)(2,1)} %get-tuple-element.67.refs_1_.refs_3_.refs_0_.refs_2_, ...), custom_call_target="tpu_custom_call" | custom-call | flops 17179869184 | bytes 67108864 | tf_op jit(solution)/shard_map/weight_grad/pallas_call | solution.py:291
  936.2 16.0 %weight_grad.14 = (bf16[1,1,1024,384]{3,2,1,0:T(8,128)(2,1)}, bf16[1,1,1024,384]{3,2,1,0:T(8,128)(2,1)}, bf16[1,1,1024,384]{3,2,1,0:T(8,128)(2,1)}, bf16[1,1,1024,384]{3,2,1,0:T(8,128)(2,1)}) custom-call(bf16[2048,2048]{1,0:T(8,128)(2,1)} %bitcast.416, bf16[2048,1536]{1,0:T(8,128)(2,1)} %bitcast.430, bf16[1,1,2048,1024]{3,2,1,0:T(8,128)(2,1)} %weight_grad.13.refs_2_), custom_call_target="tpu_custom_call" | custom-call | flops 25769803776 | bytes 92274688 | tf_op jit(solution)/shard_map/weight_grad/pallas_call | solution.py:291
  963.0 14.5 %collective-permute-done.94 = bf16[128,1024]{1,0:T(8,128)(2,1)S(1)} collective-permute-done((bf16[128,1024]{1,0:T(8,128)(2,1)S(1)}, bf16[128,1024]{1,0:T(8,128)(2,1)S(1)}, u32[]{:S(2)}, u32[]{:S(2)}) %collective-permute-start.94) | collective-permute-done | bytes 262176 | tf_op jit(solution)/shard_map/ppermute | solution.py:535
  1015.3 17.2 %weight_grad.15.refs_3_ = bf16[4,1,1024,384]{3,2,1,0:T(8,128)(2,1)} custom-call(bf16[2048,2048]{1,0:T(8,128)(2,1)} %bitcast.417, bf16[2048,1536]{1,0:T(8,128)(2,1)} %bitcast.431, bf16[1,1,1024,384]{3,2,1,0:T(8,128)(2,1)} %collective-permute-done.75.refs_2_, bf16[1,1,1024,384]{3,2,1,0:T(8,128)(2,1)} %collective-permute-done.76.refs_3_, ...), custom_call_target="tpu_custom_call" | custom-call | flops 25769803776 | bytes 92274688 | tf_op jit(solution)/shard_map/weight_grad/pallas_call | solution.py:291
  1080.9 34.3 %collective-permute-done.99 = bf16[32,1024]{1,0:T(8,128)(2,1)S(1)} collective-permute-done((bf16[32,1024]{1,0:T(8,128)(2,1)}, bf16[32,1024]{1,0:T(8,128)(2,1)S(1)}, u32[]{:S(2)}, u32[]{:S(2)}) %collective-permute-start.99) | collective-permute-done | bytes 65568 | tf_op jit(solution)/shard_map/ppermute | solution.py:535
  1184.1 14.5 %collective-permute-start.106 = (f32[49152]{0:T(1024)S(1)}, f32[49152]{0:T(1024)S(1)}, u32[]{:S(2)}, u32[]{:S(2)}) collective-permute-start(f32[49152]{0:T(1024)S(1)} %add.387), channel_id=1, source_target_pairs={{0,1},{1,0},{2,3},{3,2},{4,5},{5,4},{6,7},{7,6},{8,9},{9,8},{10,11... | collective-permute-start | bytes 589832 | tf_op jit(solution)/shard_map/ppermute | solution.py:535
  (790 shorter events, 773.0 us)
Async XLA Ops:
  7.2 91.4 %all-gather.5.cloned.1.call-start = ((), (), s32[]{:S(2)}) async-start(), calls=%async_computation.3 | async-start | bytes 3932160 | tf_op jit(solution)/shard_map/all_gather | solution.py:892
  33.5 171.8 %all-gather.7.cloned.1.call-start = ((), (), s32[]{:S(2)}) async-start(), calls=%async_computation.4 | async-start | bytes 1310720 | tf_op jit(solution)/shard_map/all_gather | solution.py:901
  38.5 60.0 %collective-permute-start.26 = (bf16[32,1024]{1,0:T(8,128)(2,1)}, bf16[32,1024]{1,0:T(8,128)(2,1)S(1)}, u32[]{:S(2)}, u32[]{:S(2)}) collective-permute-start(bf16[32,1024]{1,0:T(8,128)(2,1)} %get-tuple-element.307), channel_id=1, source_target_pairs={{0,24},{8,16},{16,8},{24,0},{1,25},{9,17},{17,9},{25,1},{2,26},{10... | collective-permute-start | bytes 196616 | tf_op jit(solution)/shard_map/ppermute | solution.py:535
  38.9 59.7 %collective-permute-start.27 = (bf16[32,1024]{1,0:T(8,128)(2,1)}, bf16[32,1024]{1,0:T(8,128)(2,1)S(1)}, u32[]{:S(2)}, u32[]{:S(2)}) collective-permute-start(bf16[32,1024]{1,0:T(8,128)(2,1)} %get-tuple-element.306), channel_id=1, source_target_pairs={{0,16},{8,24},{16,0},{24,8},{1,17},{9,25},{17,1},{25,9},{2,18},{10... | collective-permute-start | bytes 196616 | tf_op jit(solution)/shard_map/ppermute | solution.py:535
  40.5 59.3 %collective-permute-start.28 = (bf16[32,1024]{1,0:T(8,128)(2,1)}, bf16[32,1024]{1,0:T(8,128)(2,1)}, u32[]{:S(2)}, u32[]{:S(2)}) collective-permute-start(bf16[32,1024]{1,0:T(8,128)(2,1)} %get-tuple-element.305), channel_id=1, source_target_pairs={{0,8},{8,0},{16,24},{24,16},{1,9},{9,1},{17,25},{25,17},{2,10},{10... | collective-permute-start | bytes 196616 | tf_op jit(solution)/shard_map/ppermute | solution.py:535
  98.6 52.6 %collective-permute-start.12 = (bf16[4,1024,384]{2,1,0:T(8,128)(2,1)}, bf16[4,1024,384]{2,1,0:T(8,128)(2,1)}, u32[]{:S(2)}, u32[]{:S(2)}) collective-permute-start(bf16[4,1024,384]{2,1,0:T(8,128)(2,1)} %after.23.w_own.refs_1_), channel_id=1, source_target_pairs={{0,4},{4,0},{1,5},{5,1},{2,6},{6,2},{3,7},{7,3},{8,12},{12,8},{9,1... | collective-permute-start | bytes 9437192 | tf_op jit(solution)/shard_map/ppermute | solution.py:535
  103.0 198.4 %all-gather.9.cloned.1.call-start = ((), (), s32[]{:S(2)}) async-start(), calls=%async_computation.5 | async-start | bytes 10485760 | tf_op jit(solution)/shard_map/all_gather | solution.py:919
  150.7 246.4 %all-gather.11.cloned.1.call-start = ((), (), s32[]{:S(2)}) async-start(), calls=%async_computation.6 | async-start | bytes 5242880 | tf_op jit(solution)/shard_map/all_gather | solution.py:934
  316.8 590.7 %reduce-scatter.4.cloned.1.call-start = ((), (), s32[]{:S(2)}) async-start(), calls=%async_computation.7 | async-start | bytes 10485760 | tf_op jit(solution)/shard_map/reduce_scatter | solution.py:938
  602.5 59.5 %collective-permute-start.54 = (bf16[256,2048]{1,0:T(8,128)(2,1)}, bf16[256,2048]{1,0:T(8,128)(2,1)S(1)}, u32[]{:S(2)}, u32[]{:S(2)}) collective-permute-start(bf16[256,2048]{1,0:T(8,128)(2,1)} %slice.432), channel_id=1, source_target_pairs={{0,8},{8,0},{16,24},{24,16},{1,9},{9,1},{17,25},{25,17},{2,10},{10... | collective-permute-start | bytes 3145736 | tf_op jit(solution)/shard_map/ppermute | solution.py:535
  755.1 281.4 %reduce-scatter.6.cloned.1.call-start = ((), (), s32[]{:S(2)}) async-start(), calls=%async_computation.8 | async-start | bytes 5242880 | tf_op jit(solution)/shard_map/reduce_scatter | solution.py:938
  842.3 65.2 %collective-permute-start.69 = (bf16[1,1,2048,1024]{3,2,1,0:T(8,128)(2,1)}, bf16[1,1,2048,1024]{3,2,1,0:T(8,128)(2,1)}, u32[]{:S(2)}, u32[]{:S(2)}) collective-permute-start(bf16[1,1,2048,1024]{3,2,1,0:T(8,128)(2,1)} %weight_grad.9.refs_16_), channel_id=1, source_target_pairs={{0,4},{4,0},{1,5},{5,1},{2,6},{6,2},{3,7},{7,3},{8,12},{12,8},{9,1... | collective-permute-start | bytes 12582920 | tf_op jit(solution)/shard_map/ppermute | solution.py:535
  921.5 217.8 %reduce-scatter.8.cloned.1.call-start = ((), (), s32[]{:S(2)}) async-start(), calls=%async_computation.9 | async-start | bytes 3932160 | tf_op jit(solution)/shard_map/reduce_scatter | solution.py:938
  932.7 60.2 %collective-permute-start.82 = (bf16[512,512]{1,0:T(8,128)(2,1)}, bf16[512,512]{1,0:T(8,128)(2,1)S(1)}, u32[]{:S(2)}, u32[]{:S(2)}) collective-permute-start(bf16[512,512]{1,0:T(8,128)(2,1)} %get-tuple-element.246), channel_id=1, source_target_pairs={{0,24},{8,16},{16,8},{24,0},{1,25},{9,17},{17,9},{25,1},{2,26},{10... | collective-permute-start | bytes 1572872 | tf_op jit(solution)/shard_map/ppermute | solution.py:535
  934.1 59.4 %collective-permute-start.83 = (bf16[512,512]{1,0:T(8,128)(2,1)}, bf16[512,512]{1,0:T(8,128)(2,1)S(1)}, u32[]{:S(2)}, u32[]{:S(2)}) collective-permute-start(bf16[512,512]{1,0:T(8,128)(2,1)} %get-tuple-element.245), channel_id=1, source_target_pairs={{0,16},{8,24},{16,0},{24,8},{1,17},{9,25},{17,1},{25,9},{2,18},{10... | collective-permute-start | bytes 1572872 | tf_op jit(solution)/shard_map/ppermute | solution.py:535
  935.4 60.1 %collective-permute-start.84 = (bf16[512,512]{1,0:T(8,128)(2,1)}, bf16[512,512]{1,0:T(8,128)(2,1)}, u32[]{:S(2)}, u32[]{:S(2)}) collective-permute-start(bf16[512,512]{1,0:T(8,128)(2,1)} %get-tuple-element.244), channel_id=1, source_target_pairs={{0,8},{8,0},{16,24},{24,16},{1,9},{9,1},{17,25},{25,17},{2,10},{10... | collective-permute-start | bytes 1572872 | tf_op jit(solution)/shard_map/ppermute | solution.py:535
  995.5 71.8 %collective-permute-start.87 = (bf16[256,2048]{1,0:T(8,128)(2,1)}, bf16[256,2048]{1,0:T(8,128)(2,1)}, u32[]{:S(2)}, u32[]{:S(2)}) collective-permute-start(bf16[256,2048]{1,0:T(8,128)(2,1)} %get-tuple-element.243), channel_id=1, source_target_pairs={{0,16},{8,24},{16,0},{24,8},{1,17},{9,25},{17,1},{25,9},{2,18},{10... | collective-permute-start | bytes 3145736 | tf_op jit(solution)/shard_map/ppermute | solution.py:535
  1011.8 59.6 %collective-permute-start.85 = (bf16[256,2048]{1,0:T(8,128)(2,1)}, bf16[256,2048]{1,0:T(8,128)(2,1)}, u32[]{:S(2)}, u32[]{:S(2)}) collective-permute-start(bf16[256,2048]{1,0:T(8,128)(2,1)} %get-tuple-element.242), channel_id=1, source_target_pairs={{0,8},{8,0},{16,24},{24,16},{1,9},{9,1},{17,25},{25,17},{2,10},{10... | collective-permute-start | bytes 3145736 | tf_op jit(solution)/shard_map/ppermute | solution.py:535
  1013.2 61.4 %collective-permute-start.97 = (bf16[32,1024]{1,0:T(8,128)(2,1)}, bf16[32,1024]{1,0:T(8,128)(2,1)S(1)}, u32[]{:S(2)}, u32[]{:S(2)}) collective-permute-start(bf16[32,1024]{1,0:T(8,128)(2,1)} %get-tuple-element.304), channel_id=1, source_target_pairs={{0,24},{8,16},{16,8},{24,0},{1,25},{9,17},{17,9},{25,1},{2,26},{10... | collective-permute-start | bytes 196616 | tf_op jit(solution)/shard_map/ppermute | solution.py:535
  1013.8 64.8 %collective-permute-start.98 = (bf16[32,1024]{1,0:T(8,128)(2,1)}, bf16[32,1024]{1,0:T(8,128)(2,1)S(1)}, u32[]{:S(2)}, u32[]{:S(2)}) collective-permute-start(bf16[32,1024]{1,0:T(8,128)(2,1)} %get-tuple-element.303), channel_id=1, source_target_pairs={{0,16},{8,24},{16,0},{24,8},{1,17},{9,25},{17,1},{25,9},{2,18},{10... | collective-permute-start | bytes 196616 | tf_op jit(solution)/shard_map/ppermute | solution.py:535
  1066.6 54.8 %collective-permute-start.89 = (bf16[256,2048]{1,0:T(8,128)(2,1)}, bf16[256,2048]{1,0:T(8,128)(2,1)S(1)}, u32[]{:S(2)}, u32[]{:S(2)}) collective-permute-start(bf16[256,2048]{1,0:T(8,128)(2,1)} %slice.555), channel_id=1, source_target_pairs={{0,16},{8,24},{16,0},{24,8},{1,17},{9,25},{17,1},{25,9},{2,18},{10... | collective-permute-start | bytes 3145736 | tf_op jit(solution)/shard_map/ppermute | solution.py:535
  1067.3 54.1 %collective-permute-start.81 = (bf16[256,2048]{1,0:T(8,128)(2,1)}, bf16[256,2048]{1,0:T(8,128)(2,1)}, u32[]{:S(2)}, u32[]{:S(2)}) collective-permute-start(bf16[256,2048]{1,0:T(8,128)(2,1)} %slice.548), channel_id=1, source_target_pairs={{0,8},{8,0},{16,24},{24,16},{1,9},{9,1},{17,25},{25,17},{2,10},{10... | collective-permute-start | bytes 3145736 | tf_op jit(solution)/shard_map/ppermute | solution.py:535
  1115.2 90.0 %collective-permute-start.46 = (f32[512,1024]{1,0:T(8,128)}, f32[512,1024]{1,0:T(8,128)}, u32[]{:S(2)}, u32[]{:S(2)}) collective-permute-start(f32[512,1024]{1,0:T(8,128)} %get-tuple-element.228), channel_id=1, source_target_pairs={{0,4},{4,0},{1,5},{5,1},{2,6},{6,2},{3,7},{7,3},{8,12},{12,8},{9,1... | collective-permute-start | bytes 6291464 | tf_op jit(solution)/shard_map/ppermute | solution.py:535
  1139.4 69.0 %collective-permute-start.90 = (f32[512,1024]{1,0:T(8,128)}, f32[512,1024]{1,0:T(8,128)}, u32[]{:S(2)}, u32[]{:S(2)}) collective-permute-start(f32[512,1024]{1,0:T(8,128)} %get-tuple-element.216), channel_id=1, source_target_pairs={{0,4},{4,0},{1,5},{5,1},{2,6},{6,2},{3,7},{7,3},{8,12},{12,8},{9,1... | collective-permute-start | bytes 6291464 | tf_op jit(solution)/shard_map/ppermute | solution.py:535
  (227 other events, 3444.9 us)
Sparse Core Ops, SparseCore 0:
  33.6 64.8 all-gather.4
  103.2 26.5 all-gather.6
  150.8 150.5 all-gather.8
  316.9 79.0 all-gather.10
  755.2 141.9 reduce-scatter.3
  921.6 90.6 reduce-scatter.5
  1036.6 72.5 reduce-scatter.7
